TPU v7x, 32 devices: a whole 2x2x4 slice. The times are simulated.
32 devices in a mesh: lat: 8 (over z, x), lon: 4 (over y, core).
Axes of the slice: x: 2, y: 2, z: 4, core: 2. Of those that a mesh axis runs over, the one named last changes fastest.
Arguments:
- nodes: bfloat16 [8192, 256], P(('lat', 'lon')), may hold values from -6 to 6
- edges: bfloat16 [98304, 256], P(('lat', 'lon')), may hold values from -6 to 6
- senders: int32 [98304], P(('lat', 'lon')), may hold values from 0 to 767, as said below
- receivers: int32 [98304], P(('lat', 'lon')), may hold values from 0 to 255
- edge_count: int32 [32], P(('lat', 'lon')), may hold values from 1536 to 3072, as said below
- send_index: int32 [128, 64], P(('lat', 'lon')), may hold values from 0 to 255
- rim_index: int32 [64, 128], P(('lat', 'lon')), may hold values from 0 to 255
- edge_w1: bfloat16 [768, 256], replicated, may hold values from -0.21875 to 0.21875
- edge_b1: float32 [256], replicated, may hold values from -3 to 3
- edge_w2: bfloat16 [256, 256], replicated, may hold values from -0.375 to 0.375
- edge_gain: float32 [256], replicated, may hold values from 0.1 to 1.9
- node_w1: bfloat16 [512, 256], replicated, may hold values from -0.25 to 0.25
- node_b1: float32 [256], replicated, may hold values from -3 to 3
- node_w2: bfloat16 [256, 256], replicated, may hold values from -0.375 to 0.375
- node_gain: float32 [256], replicated, may hold values from 0.1 to 1.9
Outputs:
- new_nodes: bfloat16 [8192, 256], P(('lat', 'lon'))
- new_edges: bfloat16 [98304, 256], P(('lat', 'lon'))
Inputs may be any that keep to these rules, and one draw needn't show every extreme that they name: `senders`: A sender in the first band never names the slots of the band before it, one in the last band never those of the band after it. `edge_count`: some device has all 3072 slots live.
All inputs are finite; a program needn't handle non-finite values.
Results may differ from a plain program's by a relative error of at most 0.009.
Values may be sent and summed in bfloat16 or wider, within the bound.
A program may use at most 64 MiB of HBM per device.

v0:
```python
import jax
import jax.numpy as jnp
from jax import lax
from jax.sharding import PartitionSpec as P


def passed_along(block, axis, distance):
    devices = range(lax.axis_size(axis))
    route = [(i - distance, i) for i in devices if i - distance in devices]
    return lax.ppermute(block, axis, route)


def layer_norm(values, gain):
    mean = jnp.mean(values, axis=-1, keepdims=True)
    centred = values - mean
    var = jnp.mean(centred * centred, axis=-1, keepdims=True)
    return centred * lax.rsqrt(var + 1e-05) * gain


def local(
    nodes,
    edges,
    senders,
    receivers,
    edge_count,
    send_index,
    rim_index,
    edge_w1,
    edge_b1,
    edge_w2,
    edge_gain,
    node_w1,
    node_b1,
    node_w2,
    node_gain,
):
    n_lon = lax.axis_size("lon")
    node_rows, width = nodes.shape
    edge_rows = edges.shape[0]
    halo_rows = send_index.shape[1]
    band_nodes, band_lists = (
        lax.all_gather(nodes, "lon", axis=0, tiled=True),
        lax.all_gather(send_index, "lon", axis=0, tiled=True),
    )
    mine = lax.axis_index("lon")
    lists = jnp.take(band_lists.reshape(n_lon, n_lon, halo_rows), mine, axis=1)
    lists = lists + (jnp.arange(n_lon, dtype=jnp.int32) * node_rows)[:, None]
    incoming = band_nodes[lists.reshape(-1)]
    from_below = passed_along(nodes[rim_index[0]], "lat", 1)
    from_above = passed_along(nodes[rim_index[1]], "lat", -1)
    table = jnp.concatenate([nodes, incoming, from_below, from_above], axis=0)
    pre = jnp.dot(edges, edge_w1[:width], preferred_element_type=jnp.float32)
    pre = pre + jnp.dot(
        table[senders], edge_w1[width : 2 * width], preferred_element_type=jnp.float32
    )
    pre = pre + jnp.dot(nodes[receivers], edge_w1[2 * width :], preferred_element_type=jnp.float32)
    hidden = jax.nn.silu(pre + edge_b1).astype(jnp.bfloat16)
    update = layer_norm(jnp.dot(hidden, edge_w2, preferred_element_type=jnp.float32), edge_gain)
    live = jnp.arange(edge_rows, dtype=jnp.int32) < edge_count[0]
    update = jnp.where(live[:, None], update, 0.0).astype(jnp.bfloat16)
    new_edges = (edges.astype(jnp.float32) + update.astype(jnp.float32)).astype(jnp.bfloat16)
    member = (receivers[None, :] == jnp.arange(node_rows, dtype=jnp.int32)[:, None]).astype(
        jnp.bfloat16
    )
    messages = jnp.dot(member, update, preferred_element_type=jnp.float32).astype(jnp.bfloat16)
    node_pre = jnp.dot(nodes, node_w1[:width], preferred_element_type=jnp.float32)
    node_pre = node_pre + jnp.dot(messages, node_w1[width:], preferred_element_type=jnp.float32)
    node_hidden = jax.nn.silu(node_pre + node_b1).astype(jnp.bfloat16)
    node_out = layer_norm(
        jnp.dot(node_hidden, node_w2, preferred_element_type=jnp.float32), node_gain
    )
    new_nodes = (nodes.astype(jnp.float32) + node_out).astype(jnp.bfloat16)
    return (new_nodes, new_edges)


def solution(mesh):
    return jax.shard_map(
        local,
        mesh=mesh,
        in_specs=(
            P(("lat", "lon"), None),
            P(("lat", "lon"), None),
            P(("lat", "lon")),
            P(("lat", "lon")),
            P(("lat", "lon")),
            P(("lat", "lon"), None),
            P(("lat", "lon"), None),
            P(),
            P(),
            P(),
            P(),
            P(),
            P(),
            P(),
            P(),
        ),
        out_specs=(P(("lat", "lon"), None), P(("lat", "lon"), None)),
        check_vma=False,
    )
```

profile of v0, /device:TPU:0, one launch (start us, length us, event | category | flops | bytes accessed | tf_op | source)
XLA Modules:
  0.0 76.1 jit_solution(12640881311571558213)
XLA Ops:
  0.6 0.0 copy-start
  0.6 0.0 copy-start.2
  0.7 0.0 copy-start.4
  0.7 0.8 %fusion.18 = (s32[128]{0:T(128)S(1)}, s32[128]{0:T(128)S(1)}) fusion(s32[2,128]{1,0:T(2,128)} %param.21), kind=kLoop, calls=%fused_computation.48 | loop fusion | flops 768 | bytes 2048 | tf_op jit(solution)/shard_map/select_n | solution.py:49
  1.5 1.7 %gather_fusion.1 = bf16[128,256]{1,0:T(8,128)(2,1)S(1)} fusion(bf16[256,256]{1,0:T(8,128)(2,1)} %param.15, s32[1024]{0:T(1024)S(1)} %pad_clamp_fusion.1), kind=kCustom, calls=%fused_computation.1 | custom fusion | bytes 131584 | tf_op jit(solution)/shard_map/gather | solution.py:49
  3.2 4.8 %collective-permute-start = (bf16[128,256]{1,0:T(8,128)(2,1)S(1)}, bf16[128,256]{1,0:T(8,128)(2,1)S(1)}, u32[]{:S(2)}, u32[]{:S(2)}) collective-permute-start(bf16[128,256]{1,0:T(8,128)(2,1)S(1)} %gather_fusion.1), channel_id=1, source_target_pairs={{0,4},{4,8},{8,12},{12,16},{16,20},{20,24},{24,28},{1,5},{5,9},{9,... | collective-permute-start | bytes 196616 | tf_op jit(solution)/shard_map/ppermute | solution.py:10
  8.1 1.7 %gather_fusion.2 = bf16[128,256]{1,0:T(8,128)(2,1)S(1)} fusion(bf16[256,256]{1,0:T(8,128)(2,1)} %param.15, s32[1024]{0:T(1024)S(1)} %pad_clamp_fusion), kind=kCustom, calls=%fused_computation.2 | custom fusion | bytes 131584 | tf_op jit(solution)/shard_map/gather | solution.py:50
  9.8 1.3 %collective-permute-start.1 = (bf16[128,256]{1,0:T(8,128)(2,1)S(1)}, bf16[128,256]{1,0:T(8,128)(2,1)S(1)}, u32[]{:S(2)}, u32[]{:S(2)}) collective-permute-start(bf16[128,256]{1,0:T(8,128)(2,1)S(1)} %gather_fusion.2), channel_id=1, source_target_pairs={{4,0},{8,4},{12,8},{16,12},{20,16},{24,20},{28,24},{5,1},{9,5},{13... | collective-permute-start | bytes 196616 | tf_op jit(solution)/shard_map/ppermute | solution.py:10
  11.1 7.4 %all_gather.6 = bf16[1024,256]{1,0:T(8,128)(2,1)S(1)} all-gather(bf16[256,256]{1,0:T(8,128)(2,1)} %param.15), channel_id=1, replica_groups=mesh['lat'=8,'lon'=4] {'lon'}, dimensions={0}, use_global_device_ids=true | all-gather | bytes 655360 | tf_op jit(solution)/shard_map/all_gather | solution.py:42
  18.5 1.0 %copy.21 = bf16[256,256]{0,1:T(8,128)(2,1)S(1)} copy(bf16[256,256]{1,0:T(8,128)(2,1)} %param.15) | data formatting | bytes 262144 | tf_op args[0]
  19.5 5.3 %all-gather = s32[4,4,64]{2,1,0:T(4,128)S(1)} all-gather(s32[1,4,64]{2,1,0:T(4,128)} %bitcast.22), channel_id=1, replica_groups=mesh['lat'=8,'lon'=4] {'lon'}, dimensions={0}, use_global_device_ids=true | all-gather | bytes 5120 | tf_op jit(solution)/shard_map/all_gather | solution.py:43
  24.8 0.1 broadcast_add_fusion
  24.9 0.1 add.132
  25.0 0.7 fusion.16
  25.7 0.0 copy-done.2
  25.7 1.7 %copy.22 = bf16[3072,256]{0,1:T(8,128)(2,1)} copy(bf16[3072,256]{1,0:T(8,128)(2,1)S(1)} %copy-done.2) | data formatting | bytes 3145728 | tf_op args[1]
  27.4 0.0 copy-done.4
  27.4 0.0 copy-start.8
  27.4 0.0 copy-start.1
  27.4 2.2 %fusion.12 = f32[3072,256]{1,0:T(8,128)} fusion(bf16[3072,256]{1,0:T(8,128)(2,1)S(1)} %copy-done.2, bf16[768,256]{1,0:T(8,128)(2,1)S(1)} %copy-done.4), kind=kOutput, calls=%fused_computation.28 | convolution fusion | flops 402653184 | bytes 4849664 | tf_op jit(solution)/shard_map/dot_general | solution.py:52
  29.7 0.0 copy-done.8
  29.7 0.0 copy-done.1
  29.7 0.0 copy-start.6
  29.7 13.0 %gather_fusion.4 = bf16[3072,256]{1,0:T(8,128)(2,1)} fusion(bf16[256,256]{1,0:T(8,128)(2,1)S(1)} %copy-done.1, s32[3072]{0:T(1024)S(1)} %fusion.17), kind=kCustom, calls=%fused_computation.4 | custom fusion | bytes 3158016 | tf_op jit(solution)/shard_map/gather | solution.py:56
  43.4 0.0 copy-done.6
  43.4 0.9 %fusion.14 = f32[256,256]{1,0:T(8,128)} fusion(bf16[256,256]{1,0:T(8,128)(2,1)S(1)} %copy-done.1, bf16[512,256]{1,0:T(8,128)(2,1)S(1)} %copy-done.6), kind=kOutput, calls=%fused_computation.30 | convolution fusion | flops 33554432 | bytes 524288 | tf_op jit(solution)/shard_map/dot_general | solution.py:66
  44.3 1.1 %gather_fusion = bf16[256,256]{1,0:T(8,128)(2,1)S(1)} fusion(bf16[1024,256]{1,0:T(8,128)(2,1)S(1)} %all_gather.6, s32[1024]{0:T(1024)S(1)} %pad_clamp_fusion.2), kind=kCustom, calls=%fused_computation | custom fusion | bytes 263168 | tf_op jit(solution)/shard_map/gather | solution.py:48
  45.5 0.0 collective-permute-done
  45.5 0.0 collective-permute-done.1
  45.5 11.1 %gather_fusion.3 = bf16[3072,256]{1,0:T(8,128)(2,1)S(1)} fusion(bf16[768,256]{1,0:T(8,128)(2,1)S(1)} %pad_maximum_fusion, s32[3072]{0:T(1024)S(1)} %fusion.16), kind=kCustom, calls=%fused_computation.3 | custom fusion | bytes 3158016 | tf_op jit(solution)/shard_map/gather | solution.py:54
  56.6 0.0 copy-start.10
  56.6 4.1 %convolution_add_fusion.1 = f32[3072,256]{1,0:T(8,128)} fusion(f32[3072,256]{1,0:T(8,128)} %fusion.12, bf16[3072,256]{1,0:T(8,128)(2,1)S(1)} %gather_fusion.3, bf16[768,256]{1,0:T(8,128)(2,1)S(1)} %copy-done.4), kind=kOutput, calls=%fused_computation.7 | convolution fusion | flops 403439616 | bytes 7995392 | tf_op jit(solution)/shard_map/dot_general | solution.py:53
  60.7 0.0 copy-done
  60.7 0.0 copy-done.10
  60.7 3.7 %fusion.21 = (f32[3072]{0:T(1024)S(1)}, f32[3072,256]{0,1:T(8,128)S(1)}) fusion(bf16[256,256]{1,0:T(8,128)(2,1)S(1)} %copy-done, f32[3072,256]{1,0:T(8,128)} %convolution_add_fusion.1, bf16[3072,256]{1,0:T(8,128)(2,1)} %gather_fusion.4, f32[256]{0:T(256)S(1)} %copy-done.10, bf16[768,256]{1,0:T(8,128)(2,1)} %param.22), kind=kOutput, calls=%fused_computation.53 | convolution fusion | flops 811594752 | bytes 8139776 | tf_op jit(solution)/shard_map/dot_general | solution.py:58
  64.4 0.0 copy-start.3
  64.4 0.0 copy-start.9
  64.4 0.3 multiply_reduce_fusion
  64.8 1.0 %copy-done.3 = bf16[3072,256]{0,1:T(8,128)(2,1)S(1)} copy-done((bf16[3072,256]{0,1:T(8,128)(2,1)S(1)}, bf16[3072,256]{0,1:T(8,128)(2,1)}, u32[]{:S(2)}) %copy-start.3) | copy-done | bytes 1572888
  65.8 0.0 copy-done.9
  65.8 0.0 copy-start.7
  65.8 1.9 %add_convert_fusion = bf16[3072,256]{0,1:T(8,128)(2,1)} fusion(bf16[3072,256]{0,1:T(8,128)(2,1)S(1)} %copy-done.3, f32[256]{0:T(256)S(1)} %copy-done.9, f32[3072]{0:T(1024)S(1)} %add_rsqrt_fusion, f32[3072,256]{0,1:T(8,128)S(1)} %get-tuple-element.20, f32[3072]{0:T(1024)S(1)} %broadcast_multiply_fusion, pred[3072]{0:T(1024)(128)(4,1)S(1)} %iota_compare_fusion.8), kind=kLoop, calls=%fused_computation.8 | loop fusion | flops 7077888 | bytes 6320128 | tf_op jit(solution)/shard_map/convert_element_type | solution.py:61
  67.7 0.0 copy-done.7
  67.7 2.6 %copy.24 = bf16[3072,256]{1,0:T(8,128)(2,1)} copy(bf16[3072,256]{0,1:T(8,128)(2,1)} %add_convert_fusion) | data formatting | bytes 3145728
  70.3 0.0 copy-start.5
  70.3 3.0 %multiply_convert_fusion.1 = bf16[256,256]{1,0:T(8,128)(2,1)} fusion(f32[256,256]{1,0:T(8,128)} %fusion.14, s32[3072]{0:T(1024)} %param.18, f32[256]{0:T(256)} %param.27, bf16[512,256]{1,0:T(8,128)(2,1)} %param.26, f32[3072,256]{0,1:T(8,128)S(1)} %get-tuple-element.20, f32[256]{0:T(256)} %param.25, f32[3072]{0:T(1024)} %copy-done.7, ...), kind=kOutput, calls=%fused_computation.24 | convolution fusion | flops 441450496 | bytes 3712000 | tf_op jit(solution)/shard_map/dot_general | solution.py:67
  73.3 0.0 copy-done.5
  73.3 1.2 %fusion.24 = (f32[256]{0:T(256)S(1)}, f32[256,256]{0,1:T(8,128)S(1)}) fusion(bf16[256,256]{1,0:T(8,128)(2,1)} %multiply_convert_fusion.1, bf16[256,256]{1,0:T(8,128)(2,1)S(1)} %copy-done.5), kind=kOutput, calls=%fused_computation.54 | convolution fusion | flops 33619712 | bytes 525312 | tf_op jit(solution)/shard_map/dot_general | solution.py:70
  74.5 0.1 multiply_reduce_fusion.1
  74.5 0.8 %add_convert_fusion.1 = bf16[256,256]{0,1:T(8,128)(2,1)S(1)} fusion(bf16[256,256]{0,1:T(8,128)(2,1)S(1)} %copy.21, f32[256,256]{0,1:T(8,128)S(1)} %get-tuple-element.22, f32[256]{0:T(256)} %param.29, f32[256]{0:T(256)S(1)} %add_rsqrt_fusion.1, f32[256]{0:T(256)S(1)} %broadcast_multiply_fusion.1), kind=kLoop, calls=%fused_computation.22 | loop fusion | flops 393216 | bytes 527360 | tf_op jit(solution)/shard_map/convert_element_type | solution.py:72
  75.3 0.8 copy.23
  (13 shorter events, 0.1 us)
Async XLA Ops:
  0.6 60.1 %copy-start = (bf16[256,256]{1,0:T(8,128)(2,1)S(1)}, bf16[256,256]{1,0:T(8,128)(2,1)}, u32[]{:S(2)}) copy-start(bf16[256,256]{1,0:T(8,128)(2,1)} %param.24) | copy-start | bytes 393220
  0.6 25.0 %copy-start.2 = (bf16[3072,256]{1,0:T(8,128)(2,1)S(1)}, bf16[3072,256]{1,0:T(8,128)(2,1)}, u32[]{:S(2)}) copy-start(bf16[3072,256]{1,0:T(8,128)(2,1)} %param.16) | copy-start | bytes 4718596
  0.7 26.8 %copy-start.4 = (bf16[768,256]{1,0:T(8,128)(2,1)S(1)}, bf16[768,256]{1,0:T(8,128)(2,1)}, u32[]{:S(2)}) copy-start(bf16[768,256]{1,0:T(8,128)(2,1)} %param.22) | copy-start | bytes 1179652
  3.2 42.3 %collective-permute-start = (bf16[128,256]{1,0:T(8,128)(2,1)S(1)}, bf16[128,256]{1,0:T(8,128)(2,1)S(1)}, u32[]{:S(2)}, u32[]{:S(2)}) collective-permute-start(bf16[128,256]{1,0:T(8,128)(2,1)S(1)} %gather_fusion.1), channel_id=1, source_target_pairs={{0,4},{4,8},{8,12},{12,16},{16,20},{20,24},{24,28},{1,5},{5,9},{9,... | collective-permute-start | bytes 196616 | tf_op jit(solution)/shard_map/ppermute | solution.py:10
  9.8 35.7 %collective-permute-start.1 = (bf16[128,256]{1,0:T(8,128)(2,1)S(1)}, bf16[128,256]{1,0:T(8,128)(2,1)S(1)}, u32[]{:S(2)}, u32[]{:S(2)}) collective-permute-start(bf16[128,256]{1,0:T(8,128)(2,1)S(1)} %gather_fusion.2), channel_id=1, source_target_pairs={{4,0},{8,4},{12,8},{16,12},{20,16},{24,20},{28,24},{5,1},{9,5},{13... | collective-permute-start | bytes 196616 | tf_op jit(solution)/shard_map/ppermute | solution.py:10
  27.4 2.2 %copy-start.8 = (s32[3072]{0:T(1024)S(1)}, s32[3072]{0:T(1024)}, u32[]{:S(2)}) copy-start(s32[3072]{0:T(1024)} %param.18) | copy-start | bytes 36868
  27.4 2.2 %copy-start.1 = (bf16[256,256]{1,0:T(8,128)(2,1)S(1)}, bf16[256,256]{1,0:T(8,128)(2,1)}, u32[]{:S(2)}) copy-start(bf16[256,256]{1,0:T(8,128)(2,1)} %param.15) | copy-start | bytes 393220
  29.7 13.7 %copy-start.6 = (bf16[512,256]{1,0:T(8,128)(2,1)S(1)}, bf16[512,256]{1,0:T(8,128)(2,1)}, u32[]{:S(2)}) copy-start(bf16[512,256]{1,0:T(8,128)(2,1)} %param.26) | copy-start | bytes 786436
  56.6 4.1 %copy-start.10 = (f32[256]{0:T(256)S(1)}, f32[256]{0:T(256)}, u32[]{:S(2)}) copy-start(f32[256]{0:T(256)} %param.23) | copy-start | bytes 3076
  64.4 1.4 %copy-start.3 = (bf16[3072,256]{0,1:T(8,128)(2,1)S(1)}, bf16[3072,256]{0,1:T(8,128)(2,1)}, u32[]{:S(2)}) copy-start(bf16[3072,256]{0,1:T(8,128)(2,1)} %copy.22) | copy-start | bytes 4718596
  64.4 1.4 %copy-start.9 = (f32[256]{0:T(256)S(1)}, f32[256]{0:T(256)}, u32[]{:S(2)}) copy-start(f32[256]{0:T(256)} %param.25) | copy-start | bytes 3076
  65.8 1.9 %copy-start.7 = (f32[3072]{0:T(1024)}, f32[3072]{0:T(1024)S(1)}, u32[]{:S(2)}) copy-start(f32[3072]{0:T(1024)S(1)} %add_rsqrt_fusion) | copy-start | bytes 36868
  70.3 3.0 %copy-start.5 = (bf16[256,256]{1,0:T(8,128)(2,1)S(1)}, bf16[256,256]{1,0:T(8,128)(2,1)}, u32[]{:S(2)}) copy-start(bf16[256,256]{1,0:T(8,128)(2,1)} %param.28) | copy-start | bytes 393220
where the time goes:
time: 77.6 us; the launch traced here: 76.1 us
  local copies, waits for them, and re-layouts  35.8 us (46%)
  matrix products  15 us (19%)
  blocking collectives  12.7 us (16%)
  starting transfers between devices  6.14 us (8%)
  other arithmetic  4.83 us (6%)
  between operations  1.52 us (2%)
    gather x1, local copies, waits for them, and re-layouts, local(): nodes[receivers]  13 us
    gather x1, local copies, waits for them, and re-layouts, local(): table[senders]  11.1 us
    all_gather x1, blocking collectives, local(): lax.all_gather(nodes, 'lon', axis=0, tiled=True)  7.41 us
    unnamed x26, local copies, waits for them, and re-layouts  7.15 us
    ppermute x2, starting transfers between devices, passed_along(): return lax.ppermute(block, axis, route)  6.14 us
    all_gather x1, blocking collectives, local(): lax.all_gather(send_index, 'lon', axis=0, tiled=True)  5.3 us
    dot_general x1, matrix products, local(): jnp.dot(table[senders], edge_w1[width:2 * width], preferred_element_type=...  4.1 us
    dot_general x1, matrix products, local(): jnp.dot(hidden, edge_w2, preferred_element_type=jnp.float32)  3.67 us
  transfers between devices with their start and end apart: 2, of which 0 were waited for; matrix products, arithmetic and copies ran while one was open for 30% of the time, Pallas kernels for 0%

commit v1 on v0

v1 whole, which is shorter than its diff:
```python
import functools

import jax
import jax.numpy as jnp
from jax import lax
from jax.experimental import pallas as pl
from jax.experimental.pallas import tpu as pltpu
from jax.sharding import PartitionSpec as P

BF16 = jnp.bfloat16
F32 = jnp.float32
MESH = pl.DeviceIdType.MESH
LANES = 128
CHUNK = 512
AHEAD = 6


def dot(a, b):
    return jnp.dot(a, b, preferred_element_type=F32)


def lane_ids(rows):
    return lax.broadcasted_iota(jnp.int32, (rows, LANES), 1).astype(jnp.int16)


def row_ids(rows):
    return lax.broadcasted_iota(jnp.int32, (rows, LANES), 0).astype(jnp.int16)


def mark(hit):
    return jnp.where(hit, jnp.ones(hit.shape, BF16), jnp.zeros(hit.shape, BF16))


def pick_rows(columns, low, high):
    n = columns.shape[0]
    spread = jnp.broadcast_to(columns, (n, LANES)).astype(jnp.int16)
    lanes = lane_ids(n)
    tiles = [mark(spread == lanes + jnp.int16(t)) for t in range(low, high, LANES)]
    return jnp.concatenate(tiles, axis=1)


def turned(block):
    short = LANES - block.shape[0]
    if short:
        block = jnp.concatenate([block, jnp.zeros((short, LANES), jnp.int32)], axis=0)
    return jnp.transpose(block)


def centred_weights(w):
    w = w.astype(F32)
    return (w - jnp.mean(w, axis=-1, keepdims=True)).astype(BF16)


def halved_silu(h):
    return (h + h * jnp.tanh(h)).astype(BF16)


def inverse_spread(y, ones):
    return lax.rsqrt(dot((y * y).astype(BF16), ones) + 1e-05)


def kernel(
    n_lat,
    n_lon,
    count,
    senders,
    receivers,
    send_index,
    rim_index,
    b1,
    gain,
    c1,
    ngain,
    nodes_in,
    edges_in,
    w1_in,
    w2_in,
    v1_in,
    v2_in,
    new_nodes,
    new_edges,
    nodes,
    edges,
    w1,
    w2,
    v1,
    v2,
    table,
    outgoing,
    pre,
    fresh,
    fresh_nodes,
    load_sem,
    edge_sem,
    store_sem,
    send_sem,
    recv_sem,
):
    a, b = lax.axis_index("lat"), lax.axis_index("lon")
    node_rows, width = nodes.shape
    edge_rows = edges.shape[0]
    halo = send_index.shape[1]
    rim = rim_index.shape[1]
    rows = table.shape[0]
    halo_at, rim_at = node_rows, node_rows + n_lon * halo
    chunks = edge_rows // CHUNK
    blocks = CHUNK // LANES

    barrier = pltpu.get_barrier_semaphore()
    for d in range(1, n_lon):
        pl.semaphore_signal(
            barrier, inc=1, device_id=(a, lax.rem(b + d, n_lon)), device_id_type=MESH
        )

    @pl.when(a > 0)
    def _():
        pl.semaphore_signal(barrier, inc=1, device_id=(a - 1, b), device_id_type=MESH)

    @pl.when(a < n_lat - 1)
    def _():
        pl.semaphore_signal(barrier, inc=1, device_id=(a + 1, b), device_id_type=MESH)

    loads = [
        pltpu.make_async_copy(src, dst, load_sem.at[i])
        for i, (src, dst) in enumerate(
            [(nodes_in, nodes), (w1_in, w1), (w2_in, w2), (v1_in, v1), (v2_in, v2)]
        )
    ]
    edge_loads = [
        pltpu.make_async_copy(
            edges_in.at[pl.ds(i * CHUNK, CHUNK)], edges.at[pl.ds(i * CHUNK, CHUNK)], edge_sem.at[i]
        )
        for i in range(chunks)
    ]
    loads[0].start()
    loads[1].start()
    for copy in edge_loads:
        copy.start()
    for copy in loads[2:]:
        copy.start()

    lists = jnp.concatenate(
        [send_index[...], jnp.zeros((n_lon, LANES - halo), jnp.int32)], axis=1
    )
    list_turned = turned(jnp.concatenate([rim_index[...], lists], axis=0))
    sender_turned = turned(senders[...])
    receiver_turned = turned(receivers[...])

    loads[0].wait()
    loads[1].wait()
    own = nodes[...]
    table[:node_rows] = (0.5 * dot(own, w1[width : 2 * width])).astype(BF16)
    for p in range(n_lon):
        chosen = pick_rows(list_turned[:halo, 2 + p : 3 + p], 0, node_rows)
        outgoing[p * halo : (p + 1) * halo] = dot(chosen, table[:node_rows]).astype(BF16)
    for side in range(2):
        chosen = pick_rows(list_turned[:, side : side + 1], 0, node_rows)
        at = n_lon * halo + side * rim
        outgoing[at : at + rim] = dot(chosen, table[:node_rows]).astype(BF16)
    mine = pl.multiple_of(b * halo, halo)
    table[pl.ds(halo_at + mine, halo)] = outgoing[pl.ds(mine, halo)]

    @pl.when(a == 0)
    def _():
        table[rim_at : rim_at + rim] = jnp.zeros((rim, width), BF16)

    @pl.when(a == n_lat - 1)
    def _():
        table[rim_at + rim :] = jnp.zeros((rim, width), BF16)

    below = jnp.where(a > 0, 1, 0)
    above = jnp.where(a < n_lat - 1, 1, 0)
    pl.semaphore_wait(barrier, n_lon - 1 + below + above)
    band = []
    for d in range(1, n_lon):
        p = lax.rem(b + d, n_lon)
        copy = pltpu.make_async_remote_copy(
            src_ref=outgoing.at[pl.ds(pl.multiple_of(p * halo, halo), halo)],
            dst_ref=table.at[pl.ds(halo_at + mine, halo)],
            send_sem=send_sem.at[d - 1],
            recv_sem=recv_sem.at[d - 1],
            device_id=(a, p),
            device_id_type=MESH,
        )
        copy.start()
        band.append(copy)
    rims = [
        pltpu.make_async_remote_copy(
            src_ref=outgoing.at[pl.ds(n_lon * halo + side * rim, rim)],
            dst_ref=table.at[pl.ds(rim_at + side * rim, rim)],
            send_sem=send_sem.at[n_lon - 1 + side],
            recv_sem=recv_sem.at[n_lon - 1 + side],
            device_id=(a + 1 - 2 * side, b),
            device_id_type=MESH,
        )
        for side in range(2)
    ]

    @pl.when(a < n_lat - 1)
    def _():
        rims[0].start()

    @pl.when(a > 0)
    def _():
        rims[1].start()

    by_receiver = (0.5 * (dot(own, w1[2 * width :]) + b1[...])).astype(BF16)
    near = jnp.concatenate(
        [(0.5 * w1[:width].astype(F32)).astype(BF16), by_receiver, table[:node_rows]], axis=0
    )

    def near_part(i):
        edge_loads[i].wait()
        marks = []
        for j in range(i * blocks, (i + 1) * blocks):
            marks.append(
                jnp.concatenate(
                    [
                        pick_rows(receiver_turned[:, j : j + 1], 0, node_rows),
                        pick_rows(sender_turned[:, j : j + 1], 0, node_rows),
                    ],
                    axis=1,
                )
            )
        marks = jnp.concatenate(marks, axis=0)
        return dot(jnp.concatenate([edges[i * CHUNK : (i + 1) * CHUNK], marks], axis=1), near)

    for i in range(min(AHEAD, chunks)):
        pre[i * CHUNK : (i + 1) * CHUNK] = near_part(i)
    for copy in loads[2:]:
        copy.wait()
    w2c = centred_weights(w2[...])
    v2c = centred_weights(v2[...])
    ones = jnp.full((width, LANES), 1.0 / width, BF16)
    node_pre = dot(own, v1[:width]) + c1[...]

    for copy in band:
        copy.wait_recv()

    @pl.when(a > 0)
    def _():
        rims[0].wait_recv()

    @pl.when(a < n_lat - 1)
    def _():
        rims[1].wait_recv()

    far = table[node_rows:]
    live = count[0]
    messages = jnp.zeros((node_rows, width), F32)
    stores = []
    for i in range(chunks):
        span = slice(i * CHUNK, (i + 1) * CHUNK)
        marks = jnp.concatenate(
            [
                pick_rows(sender_turned[:, j : j + 1], node_rows, rows)
                for j in range(i * blocks, (i + 1) * blocks)
            ],
            axis=0,
        )
        start = pre[span] if i < AHEAD else near_part(i)
        hidden = halved_silu(start + dot(marks, far))
        y = dot(hidden, w2c)
        scale = inverse_spread(y, ones)
        slot = lax.broadcasted_iota(jnp.int32, scale.shape, 0) + i * CHUNK
        scale = jnp.where(slot < live, scale, 0.0)
        scale = jnp.concatenate([scale] * (width // LANES), axis=1)
        update = (y * scale * gain[...]).astype(BF16)
        fresh[span] = edges[span] + update
        copy = pltpu.make_async_copy(fresh.at[span], new_edges.at[span], store_sem.at[i])
        copy.start()
        stores.append(copy)
        ids = row_ids(node_rows)
        member = jnp.concatenate(
            [
                mark(
                    jnp.broadcast_to(receivers[j : j + 1], (node_rows, LANES)).astype(jnp.int16)
                    == ids
                )
                for j in range(i * blocks, (i + 1) * blocks)
            ],
            axis=1,
        )
        messages = messages + dot(member, update)

    node_pre = node_pre + dot(messages.astype(BF16), v1[width:])
    z = dot(halved_silu(0.5 * node_pre), v2c)
    scale = inverse_spread(z, ones)
    scale = jnp.concatenate([scale] * (width // LANES), axis=1)
    fresh_nodes[...] = (own.astype(F32) + z * scale * ngain[...]).astype(BF16)
    copy = pltpu.make_async_copy(fresh_nodes, new_nodes, store_sem.at[chunks])
    copy.start()
    stores.append(copy)

    for copy in band:
        copy.wait_send()

    @pl.when(a < n_lat - 1)
    def _():
        rims[0].wait_send()

    @pl.when(a > 0)
    def _():
        rims[1].wait_send()

    for copy in stores:
        copy.wait()


def local(
    n_lat,
    n_lon,
    nodes,
    edges,
    senders,
    receivers,
    edge_count,
    send_index,
    rim_index,
    edge_w1,
    edge_b1,
    edge_w2,
    edge_gain,
    node_w1,
    node_b1,
    node_w2,
    node_gain,
):
    node_rows, width = nodes.shape
    edge_rows = edges.shape[0]
    halo, rim = send_index.shape[1], rim_index.shape[1]
    listed = n_lon * halo + 2 * rim
    chunks = edge_rows // CHUNK
    vmem = pl.BlockSpec(memory_space=pltpu.VMEM)
    anywhere = pl.BlockSpec(memory_space=pl.ANY)
    return pl.pallas_call(
        functools.partial(kernel, n_lat, n_lon),
        out_shape=(
            jax.ShapeDtypeStruct(nodes.shape, BF16),
            jax.ShapeDtypeStruct(edges.shape, BF16),
        ),
        in_specs=[pl.BlockSpec(memory_space=pltpu.SMEM)] + [vmem] * 8 + [anywhere] * 6,
        out_specs=(anywhere, anywhere),
        scratch_shapes=[
            pltpu.VMEM(nodes.shape, BF16),
            pltpu.VMEM(edges.shape, BF16),
            pltpu.VMEM(edge_w1.shape, BF16),
            pltpu.VMEM(edge_w2.shape, BF16),
            pltpu.VMEM(node_w1.shape, BF16),
            pltpu.VMEM(node_w2.shape, BF16),
            pltpu.VMEM((node_rows + listed, width), BF16),
            pltpu.VMEM((listed, width), BF16),
            pltpu.VMEM((edge_rows, width), F32),
            pltpu.VMEM(edges.shape, BF16),
            pltpu.VMEM(nodes.shape, BF16),
            pltpu.SemaphoreType.DMA((5,)),
            pltpu.SemaphoreType.DMA((chunks,)),
            pltpu.SemaphoreType.DMA((chunks + 1,)),
            pltpu.SemaphoreType.DMA((n_lon + 1,)),
            pltpu.SemaphoreType.DMA((n_lon + 1,)),
        ],
        compiler_params=pltpu.CompilerParams(
            collective_id=0, has_side_effects=True, vmem_limit_bytes=48 * 1024 * 1024
        ),
    )(
        edge_count,
        senders.reshape(-1, LANES),
        receivers.reshape(-1, LANES),
        send_index,
        rim_index,
        edge_b1.reshape(1, width),
        edge_gain.reshape(1, width),
        node_b1.reshape(1, width),
        node_gain.reshape(1, width),
        nodes,
        edges,
        edge_w1,
        edge_w2,
        node_w1,
        node_w2,
    )


def solution(mesh):
    rows, flat = P(("lat", "lon"), None), P(("lat", "lon"))
    return jax.shard_map(
        functools.partial(local, mesh.shape["lat"], mesh.shape["lon"]),
        mesh=mesh,
        in_specs=(rows, rows, flat, flat, flat, rows, rows) + (P(),) * 8,
        out_specs=(rows, rows),
        check_vma=False,
    )
```

time: 77.6 us -> 27.8 us (0.36)
  the two profiles are of different devices: /device:TPU:0 before, /device:TPU:25 now
where the time goes in v1:
time: 27.8 us; the launch traced here: 27.3 us
  local copies, waits for them, and re-layouts  13.3 us (48%)
  Pallas kernels  12.6 us (45%)
  between operations  1.31 us (5%)
    unnamed x30, local copies, waits for them, and re-layouts  13.3 us
    pallas_call x1, Pallas kernels, local(): pl.pallas_call(functools.partial(kernel, n_lat, n_lon), out_shape=(jax.Sh...  12.6 us

profile of v1, /device:TPU:25, one launch (start us, length us, event | category | flops | bytes accessed | tf_op | source)
XLA Modules:
  0.0 27.3 jit_solution(9465035444601276115)
XLA Ops:
  1.3 0.0 copy-start
  1.3 1.4 %copy-done = bf16[3072,256]{1,0:T(8,128)(2,1)S(1)} copy-done((bf16[3072,256]{1,0:T(8,128)(2,1)S(1)}, bf16[3072,256]{1,0:T(8,128)(2,1)}, u32[]{:S(2)}) %copy-start) | copy-done | bytes 1572888
  2.7 0.0 copy-start.1
  2.7 1.0 %copy-done.1 = bf16[768,256]{1,0:T(8,128)(2,1)S(1)} copy-done((bf16[768,256]{1,0:T(8,128)(2,1)S(1)}, bf16[768,256]{1,0:T(8,128)(2,1)}, u32[]{:S(2)}) %copy-start.1) | copy-done | bytes 393240
  3.7 0.0 copy-start.2
  3.7 0.9 %copy-done.2 = bf16[512,256]{1,0:T(8,128)(2,1)S(1)} copy-done((bf16[512,256]{1,0:T(8,128)(2,1)S(1)}, bf16[512,256]{1,0:T(8,128)(2,1)}, u32[]{:S(2)}) %copy-start.2) | copy-done | bytes 262168
  4.6 0.0 copy-start.3
  4.6 0.9 %copy-done.3 = bf16[256,256]{1,0:T(8,128)(2,1)S(1)} copy-done((bf16[256,256]{1,0:T(8,128)(2,1)S(1)}, bf16[256,256]{1,0:T(8,128)(2,1)}, u32[]{:S(2)}) %copy-start.3) | copy-done | bytes 131096
  5.5 0.0 copy-start.4
  5.5 0.9 %copy-done.4 = bf16[256,256]{1,0:T(8,128)(2,1)S(1)} copy-done((bf16[256,256]{1,0:T(8,128)(2,1)S(1)}, bf16[256,256]{1,0:T(8,128)(2,1)}, u32[]{:S(2)}) %copy-start.4) | copy-done | bytes 131096
  6.4 0.0 copy-start.5
  6.4 0.9 %copy-done.5 = bf16[256,256]{1,0:T(8,128)(2,1)S(1)} copy-done((bf16[256,256]{1,0:T(8,128)(2,1)S(1)}, bf16[256,256]{1,0:T(8,128)(2,1)}, u32[]{:S(2)}) %copy-start.5) | copy-done | bytes 131096
  7.4 0.0 copy-start.6
  7.4 0.7 %copy-done.6 = s32[3072]{0:T(1024)S(1)} copy-done((s32[3072]{0:T(1024)S(1)}, s32[3072]{0:T(1024)}, u32[]{:S(2)}) %copy-start.6) | copy-done | bytes 12312
  8.1 0.0 copy-start.7
  8.1 0.7 %copy-done.7 = s32[3072]{0:T(1024)S(1)} copy-done((s32[3072]{0:T(1024)S(1)}, s32[3072]{0:T(1024)}, u32[]{:S(2)}) %copy-start.7) | copy-done | bytes 12312
  8.8 0.0 copy-start.8
  8.8 0.7 %copy-done.8 = s32[4,64]{1,0:T(4,128)S(1)} copy-done((s32[4,64]{1,0:T(4,128)S(1)}, s32[4,64]{1,0:T(4,128)}, u32[]{:S(2)}) %copy-start.8) | copy-done | bytes 1048
  9.4 0.0 copy-start.9
  9.5 0.7 %copy-done.9 = s32[2,128]{1,0:T(2,128)S(1)} copy-done((s32[2,128]{1,0:T(2,128)S(1)}, s32[2,128]{1,0:T(2,128)}, u32[]{:S(2)}) %copy-start.9) | copy-done | bytes 1048
  10.1 0.0 copy-start.10
  10.1 0.7 %copy-done.10 = f32[256]{0:T(256)S(1)} copy-done((f32[256]{0:T(256)S(1)}, f32[256]{0:T(256)}, u32[]{:S(2)}) %copy-start.10) | copy-done | bytes 1048
  10.8 0.0 copy-start.11
  10.8 0.7 %copy-done.11 = f32[256]{0:T(256)S(1)} copy-done((f32[256]{0:T(256)S(1)}, f32[256]{0:T(256)}, u32[]{:S(2)}) %copy-start.11) | copy-done | bytes 1048
  11.5 0.0 copy-start.12
  11.5 0.7 %copy-done.12 = f32[256]{0:T(256)S(1)} copy-done((f32[256]{0:T(256)S(1)}, f32[256]{0:T(256)}, u32[]{:S(2)}) %copy-start.12) | copy-done | bytes 1048
  12.2 0.0 copy-start.13
  12.2 0.7 %copy-done.13 = f32[256]{0:T(256)S(1)} copy-done((f32[256]{0:T(256)S(1)}, f32[256]{0:T(256)}, u32[]{:S(2)}) %copy-start.13) | copy-done | bytes 1048
  12.8 12.6 %shard_map.158 = (bf16[256,256]{1,0:T(8,128)(2,1)S(1)}, bf16[3072,256]{1,0:T(8,128)(2,1)S(1)}) custom-call(s32[1]{0:T(128)S(6)} %copy.19.count, s32[24,128]{1,0:T(8,128)S(1)} %bitcast.6, s32[24,128]{1,0:T(8,128)S(1)} %bitcast.7, s32[4,64]{1,0:T(4,128)S(1)} %copy-done.8, s32[2,128]{1,0:T(2,128)S(1)} %copy-done.9, f32[1,256]{1,0:T(1,128)S(1)} %bitcast.8, ...), custom_call_target="tpu_custom_call" | custom-call | tf_op jit(solution)/shard_map/pallas_call | solution.py:336
  25.5 0.7 %copy.20 = bf16[256,256]{1,0:T(8,128)(2,1)} copy(bf16[256,256]{1,0:T(8,128)(2,1)S(1)} %get-tuple-element.4) | data formatting | bytes 262144
  26.1 1.1 %copy.21 = bf16[3072,256]{1,0:T(8,128)(2,1)} copy(bf16[3072,256]{1,0:T(8,128)(2,1)S(1)} %get-tuple-element.5) | data formatting | bytes 3145728
Async XLA Ops:
  1.3 1.4 %copy-start = (bf16[3072,256]{1,0:T(8,128)(2,1)S(1)}, bf16[3072,256]{1,0:T(8,128)(2,1)}, u32[]{:S(2)}) copy-start(bf16[3072,256]{1,0:T(8,128)(2,1)} %edges_in.1) | copy-start | bytes 4718596
  2.7 1.0 %copy-start.1 = (bf16[768,256]{1,0:T(8,128)(2,1)S(1)}, bf16[768,256]{1,0:T(8,128)(2,1)}, u32[]{:S(2)}) copy-start(bf16[768,256]{1,0:T(8,128)(2,1)} %w1_in.1) | copy-start | bytes 1179652
  3.7 0.9 %copy-start.2 = (bf16[512,256]{1,0:T(8,128)(2,1)S(1)}, bf16[512,256]{1,0:T(8,128)(2,1)}, u32[]{:S(2)}) copy-start(bf16[512,256]{1,0:T(8,128)(2,1)} %v1_in.1) | copy-start | bytes 786436
  4.6 0.9 %copy-start.3 = (bf16[256,256]{1,0:T(8,128)(2,1)S(1)}, bf16[256,256]{1,0:T(8,128)(2,1)}, u32[]{:S(2)}) copy-start(bf16[256,256]{1,0:T(8,128)(2,1)} %nodes_in.1) | copy-start | bytes 393220
  5.5 0.9 %copy-start.4 = (bf16[256,256]{1,0:T(8,128)(2,1)S(1)}, bf16[256,256]{1,0:T(8,128)(2,1)}, u32[]{:S(2)}) copy-start(bf16[256,256]{1,0:T(8,128)(2,1)} %w2_in.1) | copy-start | bytes 393220
  6.4 0.9 %copy-start.5 = (bf16[256,256]{1,0:T(8,128)(2,1)S(1)}, bf16[256,256]{1,0:T(8,128)(2,1)}, u32[]{:S(2)}) copy-start(bf16[256,256]{1,0:T(8,128)(2,1)} %v2_in.1) | copy-start | bytes 393220
  7.4 0.7 %copy-start.6 = (s32[3072]{0:T(1024)S(1)}, s32[3072]{0:T(1024)}, u32[]{:S(2)}) copy-start(s32[3072]{0:T(1024)} %param.17) | copy-start | bytes 36868
  8.1 0.7 %copy-start.7 = (s32[3072]{0:T(1024)S(1)}, s32[3072]{0:T(1024)}, u32[]{:S(2)}) copy-start(s32[3072]{0:T(1024)} %param.18) | copy-start | bytes 36868
  8.8 0.7 %copy-start.8 = (s32[4,64]{1,0:T(4,128)S(1)}, s32[4,64]{1,0:T(4,128)}, u32[]{:S(2)}) copy-start(s32[4,64]{1,0:T(4,128)} %send_index.1) | copy-start | bytes 3076
  9.4 0.7 %copy-start.9 = (s32[2,128]{1,0:T(2,128)S(1)}, s32[2,128]{1,0:T(2,128)}, u32[]{:S(2)}) copy-start(s32[2,128]{1,0:T(2,128)} %rim_index.1) | copy-start | bytes 3076
  10.1 0.7 %copy-start.10 = (f32[256]{0:T(256)S(1)}, f32[256]{0:T(256)}, u32[]{:S(2)}) copy-start(f32[256]{0:T(256)} %param.23) | copy-start | bytes 3076
  10.8 0.7 %copy-start.11 = (f32[256]{0:T(256)S(1)}, f32[256]{0:T(256)}, u32[]{:S(2)}) copy-start(f32[256]{0:T(256)} %param.25) | copy-start | bytes 3076
  11.5 0.7 %copy-start.12 = (f32[256]{0:T(256)S(1)}, f32[256]{0:T(256)}, u32[]{:S(2)}) copy-start(f32[256]{0:T(256)} %param.27) | copy-start | bytes 3076
  12.2 0.7 %copy-start.13 = (f32[256]{0:T(256)S(1)}, f32[256]{0:T(256)}, u32[]{:S(2)}) copy-start(f32[256]{0:T(256)} %param.29) | copy-start | bytes 3076

commit v2 on v1

--- a/solution.py
+++ b/solution.py
@@ -63,35 +63,42 @@
     n_lat,
     n_lon,
     count,
+    nodes_in,
+    w1_in,
+    send_index_in,
+    rim_index_in,
+    senders_in,
+    receivers_in,
+    b1_in,
+    gain_in,
+    c1_in,
+    ngain_in,
+    w2_in,
+    v1_in,
+    v2_in,
+    edges_in,
+    new_nodes,
+    new_edges,
+    nodes,
+    w1,
+    send_index,
+    rim_index,
     senders,
     receivers,
-    send_index,
-    rim_index,
     b1,
     gain,
     c1,
     ngain,
-    nodes_in,
-    edges_in,
-    w1_in,
-    w2_in,
-    v1_in,
-    v2_in,
-    new_nodes,
-    new_edges,
-    nodes,
-    edges,
-    w1,
     w2,
     v1,
     v2,
+    edges,
     table,
     outgoing,
     pre,
     fresh,
     fresh_nodes,
     load_sem,
-    edge_sem,
     store_sem,
     send_sem,
     recv_sem,
@@ -120,34 +127,34 @@
     def _():
         pl.semaphore_signal(barrier, inc=1, device_id=(a + 1, b), device_id_type=MESH)
 
+    pairs = [
+        (nodes_in, nodes),
+        (w1_in, w1),
+        (send_index_in, send_index),
+        (rim_index_in, rim_index),
+        (senders_in, senders),
+        (receivers_in, receivers),
+        (b1_in, b1),
+        (gain_in, gain),
+        (c1_in, c1),
+        (ngain_in, ngain),
+        (w2_in, w2),
+        (v1_in, v1),
+        (v2_in, v2),
+        (edges_in, edges),
+    ]
     loads = [
-        pltpu.make_async_copy(src, dst, load_sem.at[i])
-        for i, (src, dst) in enumerate(
-            [(nodes_in, nodes), (w1_in, w1), (w2_in, w2), (v1_in, v1), (v2_in, v2)]
-        )
+        pltpu.make_async_copy(src, dst, load_sem.at[i]) for i, (src, dst) in enumerate(pairs)
     ]
-    edge_loads = [
-        pltpu.make_async_copy(
-            edges_in.at[pl.ds(i * CHUNK, CHUNK)], edges.at[pl.ds(i * CHUNK, CHUNK)], edge_sem.at[i]
-        )
-        for i in range(chunks)
-    ]
-    loads[0].start()
-    loads[1].start()
-    for copy in edge_loads:
+    for copy in loads:
         copy.start()
-    for copy in loads[2:]:
-        copy.start()
+    for copy in loads[:4]:
+        copy.wait()
 
     lists = jnp.concatenate(
         [send_index[...], jnp.zeros((n_lon, LANES - halo), jnp.int32)], axis=1
     )
     list_turned = turned(jnp.concatenate([rim_index[...], lists], axis=0))
-    sender_turned = turned(senders[...])
-    receiver_turned = turned(receivers[...])
-
-    loads[0].wait()
-    loads[1].wait()
     own = nodes[...]
     table[:node_rows] = (0.5 * dot(own, w1[width : 2 * width])).astype(BF16)
     for p in range(n_lon):
@@ -204,13 +211,16 @@
     def _():
         rims[1].start()
 
+    for copy in loads[4:]:
+        copy.wait()
+    sender_turned = turned(senders[...])
+    receiver_turned = turned(receivers[...])
     by_receiver = (0.5 * (dot(own, w1[2 * width :]) + b1[...])).astype(BF16)
     near = jnp.concatenate(
         [(0.5 * w1[:width].astype(F32)).astype(BF16), by_receiver, table[:node_rows]], axis=0
     )
 
     def near_part(i):
-        edge_loads[i].wait()
         marks = []
         for j in range(i * blocks, (i + 1) * blocks):
             marks.append(
@@ -227,8 +237,6 @@
 
     for i in range(min(AHEAD, chunks)):
         pre[i * CHUNK : (i + 1) * CHUNK] = near_part(i)
-    for copy in loads[2:]:
-        copy.wait()
     w2c = centred_weights(w2[...])
     v2c = centred_weights(v2[...])
     ones = jnp.full((width, LANES), 1.0 / width, BF16)
@@ -331,54 +339,47 @@
     halo, rim = send_index.shape[1], rim_index.shape[1]
     listed = n_lon * halo + 2 * rim
     chunks = edge_rows // CHUNK
-    vmem = pl.BlockSpec(memory_space=pltpu.VMEM)
-    anywhere = pl.BlockSpec(memory_space=pl.ANY)
+    operands = (
+        nodes,
+        edge_w1,
+        send_index,
+        rim_index,
+        senders.reshape(-1, LANES),
+        receivers.reshape(-1, LANES),
+        edge_b1.reshape(1, width),
+        edge_gain.reshape(1, width),
+        node_b1.reshape(1, width),
+        node_gain.reshape(1, width),
+        edge_w2,
+        node_w1,
+        node_w2,
+        edges,
+    )
+    hbm = pl.BlockSpec(memory_space=pltpu.HBM)
     return pl.pallas_call(
         functools.partial(kernel, n_lat, n_lon),
         out_shape=(
             jax.ShapeDtypeStruct(nodes.shape, BF16),
             jax.ShapeDtypeStruct(edges.shape, BF16),
         ),
-        in_specs=[pl.BlockSpec(memory_space=pltpu.SMEM)] + [vmem] * 8 + [anywhere] * 6,
-        out_specs=(anywhere, anywhere),
-        scratch_shapes=[
-            pltpu.VMEM(nodes.shape, BF16),
-            pltpu.VMEM(edges.shape, BF16),
-            pltpu.VMEM(edge_w1.shape, BF16),
-            pltpu.VMEM(edge_w2.shape, BF16),
-            pltpu.VMEM(node_w1.shape, BF16),
-            pltpu.VMEM(node_w2.shape, BF16),
+        in_specs=[pl.BlockSpec(memory_space=pltpu.SMEM)] + [hbm] * len(operands),
+        out_specs=(hbm, hbm),
+        scratch_shapes=[pltpu.VMEM(x.shape, x.dtype) for x in operands]
+        + [
             pltpu.VMEM((node_rows + listed, width), BF16),
             pltpu.VMEM((listed, width), BF16),
             pltpu.VMEM((edge_rows, width), F32),
             pltpu.VMEM(edges.shape, BF16),
             pltpu.VMEM(nodes.shape, BF16),
-            pltpu.SemaphoreType.DMA((5,)),
-            pltpu.SemaphoreType.DMA((chunks,)),
+            pltpu.SemaphoreType.DMA((len(operands),)),
             pltpu.SemaphoreType.DMA((chunks + 1,)),
             pltpu.SemaphoreType.DMA((n_lon + 1,)),
             pltpu.SemaphoreType.DMA((n_lon + 1,)),
         ],
         compiler_params=pltpu.CompilerParams(
-            collective_id=0, has_side_effects=True, vmem_limit_bytes=48 * 1024 * 1024
+            collective_id=0, has_side_effects=True, vmem_limit_bytes=60 * 1024 * 1024
         ),
-    )(
-        edge_count,
-        senders.reshape(-1, LANES),
-        receivers.reshape(-1, LANES),
-        send_index,
-        rim_index,
-        edge_b1.reshape(1, width),
-        edge_gain.reshape(1, width),
-        node_b1.reshape(1, width),
-        node_gain.reshape(1, width),
-        nodes,
-        edges,
-        edge_w1,
-        edge_w2,
-        node_w1,
-        node_w2,
-    )
+    )(edge_count, *operands)
 
 
 def solution(mesh):

time: 27.8 us -> 17.9 us (0.64)
  the two profiles are of different devices: /device:TPU:25 before, /device:TPU:0 now
where the time goes in v2:
time: 17.9 us; the launch traced here: 17.7 us
  Pallas kernels  12.2 us (68%)
  local copies, waits for them, and re-layouts  4.22 us (24%)
  between operations  1.29 us (7%)
    pallas_call x1, Pallas kernels, local(): pl.pallas_call(functools.partial(kernel, n_lat, n_lon), out_shape=(jax.Sh...  12.2 us
    unnamed x2, local copies, waits for them, and re-layouts  4.22 us

profile of v2, /device:TPU:0, one launch (start us, length us, event | category | flops | bytes accessed | tf_op | source)
XLA Modules:
  0.0 17.7 jit_solution(11495481371821933688)
XLA Ops:
  1.3 12.2 %shard_map.158 = (bf16[256,256]{1,0:T(8,128)(2,1)}, bf16[3072,256]{1,0:T(8,128)(2,1)}) custom-call(s32[1]{0:T(128)S(6)} %copy.19.count, bf16[256,256]{1,0:T(8,128)(2,1)} %nodes_in.1, bf16[768,256]{1,0:T(8,128)(2,1)} %w1_in.1, s32[4,64]{1,0:T(4,128)} %send_index_in.1, s32[2,128]{1,0:T(2,128)} %rim_index_in.1, s32[24,128]{1,0:T(8,128)} %bitcast.6, ...), custom_call_target="tpu_custom_call" | custom-call | tf_op jit(solution)/shard_map/pallas_call | solution.py:359
  13.5 1.6 %copy.20 = bf16[256,256]{1,0:T(8,128)(2,1)} copy(bf16[256,256]{1,0:T(8,128)(2,1)} %get-tuple-element.4) | data formatting | bytes 262144
  15.0 2.7 %copy.21 = bf16[3072,256]{1,0:T(8,128)(2,1)} copy(bf16[3072,256]{1,0:T(8,128)(2,1)} %get-tuple-element.5) | data formatting | bytes 3145728

commit v3 on v2

v3 whole, which is shorter than its diff:
```python
import functools

import jax
import jax.numpy as jnp
from jax import lax
from jax.experimental import pallas as pl
from jax.experimental.pallas import tpu as pltpu
from jax.sharding import PartitionSpec as P

BF16 = jnp.bfloat16
F32 = jnp.float32
MESH = pl.DeviceIdType.MESH
LANES = 128
CHUNK = 512


def dot(a, b):
    return jnp.dot(a, b, preferred_element_type=F32)


def lane_ids(rows):
    return lax.broadcasted_iota(jnp.int32, (rows, LANES), 1).astype(jnp.int16)


def row_ids(rows):
    return lax.broadcasted_iota(jnp.int32, (rows, LANES), 0).astype(jnp.int16)


def mark(hit):
    return jnp.where(hit, jnp.ones(hit.shape, BF16), jnp.zeros(hit.shape, BF16))


def pick_rows(columns, low, high):
    n = columns.shape[0]
    spread = jnp.broadcast_to(columns, (n, LANES)).astype(jnp.int16)
    lanes = lane_ids(n)
    tiles = [mark(spread == lanes + jnp.int16(t)) for t in range(low, high, LANES)]
    return jnp.concatenate(tiles, axis=1)


def turned(block):
    short = LANES - block.shape[0]
    if short:
        block = jnp.concatenate([block, jnp.zeros((short, LANES), jnp.int32)], axis=0)
    return jnp.transpose(block)


def centred_weights(w):
    w = w.astype(F32)
    return (w - jnp.mean(w, axis=-1, keepdims=True)).astype(BF16)


def halved_silu(h):
    return (h + h * jnp.tanh(h)).astype(BF16)


def inverse_spread(y, ones):
    return lax.rsqrt(dot((y * y).astype(BF16), ones) + 1e-05)


def exchange(
    n_lat,
    n_lon,
    nodes_in,
    w1_in,
    send_index_in,
    rim_index_in,
    senders_in,
    b1_in,
    c1_in,
    w2_in,
    v2_in,
    receivers_in,
    gain_in,
    ngain_in,
    v1_in,
    edges_in,
    far,
    pre,
    node_pre,
    w2c,
    v2c,
    sender_turned,
    nodes,
    receivers,
    gain,
    ngain,
    v1,
    edges,
    w1,
    send_index,
    rim_index,
    senders,
    b1,
    c1,
    w2,
    v2,
    outgoing,
    load_sem,
    send_sem,
    recv_sem,
):
    a, b = lax.axis_index("lat"), lax.axis_index("lon")
    node_rows, width = nodes.shape
    halo = send_index.shape[1]
    rim = rim_index.shape[1]
    rim_at = n_lon * halo
    chunks = edges.shape[0] // CHUNK
    blocks = CHUNK // LANES

    barrier = pltpu.get_barrier_semaphore()
    for d in range(1, n_lon):
        pl.semaphore_signal(
            barrier, inc=1, device_id=(a, lax.rem(b + d, n_lon)), device_id_type=MESH
        )

    @pl.when(a > 0)
    def _():
        pl.semaphore_signal(barrier, inc=1, device_id=(a - 1, b), device_id_type=MESH)

    @pl.when(a < n_lat - 1)
    def _():
        pl.semaphore_signal(barrier, inc=1, device_id=(a + 1, b), device_id_type=MESH)

    pairs = [
        (nodes_in, nodes),
        (w1_in, w1),
        (send_index_in, send_index),
        (rim_index_in, rim_index),
        (senders_in, senders),
        (b1_in, b1),
        (c1_in, c1),
        (w2_in, w2),
        (v2_in, v2),
        (receivers_in, receivers),
        (gain_in, gain),
        (ngain_in, ngain),
        (v1_in, v1),
        (edges_in, edges),
    ]
    loads = [
        pltpu.make_async_copy(src, dst, load_sem.at[i]) for i, (src, dst) in enumerate(pairs)
    ]
    for copy in loads:
        copy.start()
    for copy in loads[:4]:
        copy.wait()

    lists = jnp.concatenate(
        [send_index[...], jnp.zeros((n_lon, LANES - halo), jnp.int32)], axis=1
    )
    list_turned = turned(jnp.concatenate([rim_index[...], lists], axis=0))
    own = nodes[...]
    by_sender = (0.5 * dot(own, w1[width : 2 * width])).astype(BF16)
    for p in range(n_lon):
        chosen = pick_rows(list_turned[:halo, 2 + p : 3 + p], 0, node_rows)
        outgoing[p * halo : (p + 1) * halo] = dot(chosen, by_sender).astype(BF16)
    for side in range(2):
        chosen = pick_rows(list_turned[:, side : side + 1], 0, node_rows)
        at = n_lon * halo + side * rim
        outgoing[at : at + rim] = dot(chosen, by_sender).astype(BF16)
    mine = pl.multiple_of(b * halo, halo)
    far[pl.ds(mine, halo)] = outgoing[pl.ds(mine, halo)]

    @pl.when(a == 0)
    def _():
        far[rim_at : rim_at + rim] = jnp.zeros((rim, width), BF16)

    @pl.when(a == n_lat - 1)
    def _():
        far[rim_at + rim :] = jnp.zeros((rim, width), BF16)

    below = jnp.where(a > 0, 1, 0)
    above = jnp.where(a < n_lat - 1, 1, 0)
    pl.semaphore_wait(barrier, n_lon - 1 + below + above)
    band = []
    for d in range(1, n_lon):
        p = lax.rem(b + d, n_lon)
        copy = pltpu.make_async_remote_copy(
            src_ref=outgoing.at[pl.ds(pl.multiple_of(p * halo, halo), halo)],
            dst_ref=far.at[pl.ds(mine, halo)],
            send_sem=send_sem.at[d - 1],
            recv_sem=recv_sem.at[d - 1],
            device_id=(a, p),
            device_id_type=MESH,
        )
        copy.start()
        band.append(copy)
    rims = [
        pltpu.make_async_remote_copy(
            src_ref=outgoing.at[pl.ds(n_lon * halo + side * rim, rim)],
            dst_ref=far.at[pl.ds(rim_at + side * rim, rim)],
            send_sem=send_sem.at[n_lon - 1 + side],
            recv_sem=recv_sem.at[n_lon - 1 + side],
            device_id=(a + 1 - 2 * side, b),
            device_id_type=MESH,
        )
        for side in range(2)
    ]

    @pl.when(a < n_lat - 1)
    def _():
        rims[0].start()

    @pl.when(a > 0)
    def _():
        rims[1].start()

    for copy in loads[4:]:
        copy.wait()
    sender_turned[...] = turned(senders[...])
    receiver_turned = turned(receivers[...])
    by_receiver = (0.5 * (dot(own, w1[2 * width :]) + b1[...])).astype(BF16)
    near = jnp.concatenate(
        [(0.5 * w1[:width].astype(F32)).astype(BF16), by_receiver, by_sender], axis=0
    )
    for i in range(chunks):
        span = slice(i * CHUNK, (i + 1) * CHUNK)
        marks = [
            jnp.concatenate(
                [
                    pick_rows(receiver_turned[:, j : j + 1], 0, node_rows),
                    pick_rows(sender_turned[:, j : j + 1], 0, node_rows),
                ],
                axis=1,
            )
            for j in range(i * blocks, (i + 1) * blocks)
        ]
        marks = jnp.concatenate(marks, axis=0)
        pre[span] = dot(jnp.concatenate([edges[span], marks], axis=1), near)
    w2c[...] = centred_weights(w2[...])
    v2c[...] = centred_weights(v2[...])
    node_pre[...] = 0.5 * (dot(own, v1[:width]) + c1[...])

    for copy in band:
        copy.wait()

    @pl.when(a < n_lat - 1)
    def _():
        rims[0].wait_send()
        rims[1].wait_recv()

    @pl.when(a > 0)
    def _():
        rims[1].wait_send()
        rims[0].wait_recv()


def finish(
    count,
    far,
    pre,
    node_pre,
    w2c,
    v2c,
    sender_turned,
    nodes,
    receivers,
    gain,
    ngain,
    v1,
    edges,
    new_nodes,
    new_edges,
    fresh,
    fresh_nodes,
    store_sem,
):
    node_rows, width = nodes.shape
    chunks = edges.shape[0] // CHUNK
    blocks = CHUNK // LANES
    ones = jnp.full((width, LANES), 1.0 / width, BF16)
    live = count[0]
    messages = jnp.zeros((node_rows, width), F32)
    ids = row_ids(node_rows)
    stores = []
    for i in range(chunks):
        span = slice(i * CHUNK, (i + 1) * CHUNK)
        marks = [
            pick_rows(sender_turned[:, j : j + 1], node_rows, node_rows + far.shape[0])
            for j in range(i * blocks, (i + 1) * blocks)
        ]
        hidden = halved_silu(pre[span] + dot(jnp.concatenate(marks, axis=0), far[...]))
        y = dot(hidden, w2c[...])
        scale = inverse_spread(y, ones)
        slot = lax.broadcasted_iota(jnp.int32, scale.shape, 0) + i * CHUNK
        scale = jnp.where(slot < live, scale, 0.0)
        scale = jnp.concatenate([scale] * (width // LANES), axis=1)
        update = (y * scale * gain[...]).astype(BF16)
        fresh[span] = edges[span] + update
        copy = pltpu.make_async_copy(fresh.at[span], new_edges.at[span], store_sem.at[i])
        copy.start()
        stores.append(copy)
        member = [
            mark(jnp.broadcast_to(receivers[j : j + 1], ids.shape).astype(jnp.int16) == ids)
            for j in range(i * blocks, (i + 1) * blocks)
        ]
        messages = messages + dot(jnp.concatenate(member, axis=1), update)

    h = node_pre[...] + 0.5 * dot(messages.astype(BF16), v1[width:])
    z = dot(halved_silu(h), v2c[...])
    scale = inverse_spread(z, ones)
    scale = jnp.concatenate([scale] * (width // LANES), axis=1)
    fresh_nodes[...] = (nodes[...].astype(F32) + z * scale * ngain[...]).astype(BF16)
    copy = pltpu.make_async_copy(fresh_nodes, new_nodes, store_sem.at[chunks])
    copy.start()
    for copy in stores + [copy]:
        copy.wait()


def in_hbm(x):
    return pltpu.with_memory_space_constraint(x, pltpu.HBM)


def local(
    n_lat,
    n_lon,
    nodes,
    edges,
    senders,
    receivers,
    edge_count,
    send_index,
    rim_index,
    edge_w1,
    edge_b1,
    edge_w2,
    edge_gain,
    node_w1,
    node_b1,
    node_w2,
    node_gain,
):
    width = nodes.shape[1]
    listed = n_lon * send_index.shape[1] + 2 * rim_index.shape[1]
    inner = (
        nodes,
        edge_w1,
        send_index,
        rim_index,
        senders.reshape(-1, LANES),
        edge_b1.reshape(1, width),
        node_b1.reshape(1, width),
        edge_w2,
        node_w2,
    )
    passed = (
        receivers.reshape(-1, LANES),
        edge_gain.reshape(1, width),
        node_gain.reshape(1, width),
        node_w1,
        edges,
    )
    operands = [in_hbm(x) for x in inner + passed]
    handed = [
        ((listed, width), BF16),
        (edges.shape, F32),
        (nodes.shape, F32),
        (edge_w2.shape, BF16),
        (node_w2.shape, BF16),
        ((LANES, LANES), jnp.int32),
        (nodes.shape, BF16),
    ] + [(x.shape, x.dtype) for x in passed]
    hbm = pl.BlockSpec(memory_space=pltpu.HBM)
    vmem = pl.BlockSpec(memory_space=pltpu.VMEM)
    limit = 24 * 1024 * 1024
    between = pl.pallas_call(
        functools.partial(exchange, n_lat, n_lon),
        out_shape=tuple(pltpu.VMEM(shape, dtype) for shape, dtype in handed),
        in_specs=[hbm] * len(operands),
        out_specs=(vmem,) * len(handed),
        scratch_shapes=[pltpu.VMEM(x.shape, x.dtype) for x in inner[1:]]
        + [
            pltpu.VMEM((listed, width), BF16),
            pltpu.SemaphoreType.DMA((len(operands),)),
            pltpu.SemaphoreType.DMA((n_lon + 1,)),
            pltpu.SemaphoreType.DMA((n_lon + 1,)),
        ],
        compiler_params=pltpu.CompilerParams(
            collective_id=0, has_side_effects=True, vmem_limit_bytes=limit
        ),
    )(*operands)
    chunks = edges.shape[0] // CHUNK
    return pl.pallas_call(
        finish,
        out_shape=(pltpu.HBM(nodes.shape, BF16), pltpu.HBM(edges.shape, BF16)),
        in_specs=[pl.BlockSpec(memory_space=pltpu.SMEM)] + [vmem] * len(handed),
        out_specs=(hbm, hbm),
        scratch_shapes=[
            pltpu.VMEM(edges.shape, BF16),
            pltpu.VMEM(nodes.shape, BF16),
            pltpu.SemaphoreType.DMA((chunks + 1,)),
        ],
        compiler_params=pltpu.CompilerParams(vmem_limit_bytes=limit),
    )(edge_count, *between)


def solution(mesh):
    rows, flat = P(("lat", "lon"), None), P(("lat", "lon"))
    return jax.shard_map(
        functools.partial(local, mesh.shape["lat"], mesh.shape["lon"]),
        mesh=mesh,
        in_specs=(rows, rows, flat, flat, flat, rows, rows) + (P(),) * 8,
        out_specs=(rows, rows),
        check_vma=False,
    )
```

time: 17.9 us -> 13.1 us (0.73)
  local copies, waits for them, and re-layouts: 4.22 us -> 0 us
  Pallas kernels: 12.2 us -> 11.6 us
    unnamed x2 -> x0, local copies, waits for them, and re-layouts: 4.22 us -> none
    pallas_call x1 -> x2, Pallas kernels: 12.2 us -> 11.6 us  [the longest x1 7.12 us: local(): pl.pallas_call(functools.partial(exchange, n_lat, n_lon), out_shape=tuple...]
where the time goes in v3:
time: 13.1 us; the launch traced here: 12.9 us
  Pallas kernels  11.6 us (89%)
  between operations  1.29 us (10%)
    pallas_call x1, Pallas kernels, local(): pl.pallas_call(functools.partial(exchange, n_lat, n_lon), out_shape=tuple...  7.12 us
    pallas_call x1, Pallas kernels, local(): pl.pallas_call(finish, out_shape=(pltpu.HBM(nodes.shape, BF16), pltpu.HBM...  4.44 us

profile of v3, /device:TPU:0, one launch (start us, length us, event | category | flops | bytes accessed | tf_op | source)
XLA Modules:
  0.0 12.9 jit_solution(13411985941586707357)
XLA Ops:
  1.3 7.1 %shard_map.158 = (bf16[512,256]{1,0:T(8,128)(2,1)S(1)}, f32[3072,256]{1,0:T(8,128)S(1)}, f32[256,256]{1,0:T(8,128)S(1)}, bf16[256,256]{1,0:T(8,128)(2,1)S(1)}, b...) custom-call(bf16[256,256]{1,0:T(8,128)(2,1)} %nodes_in.1, ...), custom_call_target="tpu_custom_call" | custom-call | tf_op jit(solution)/shard_map/pallas_call | solution.py:367
  8.4 4.4 %shard_map.159 = (bf16[256,256]{1,0:T(8,128)(2,1)}, bf16[3072,256]{1,0:T(8,128)(2,1)}) custom-call(s32[1]{0:T(128)S(6)} %copy.17.count, bf16[512,256]{1,0:T(8,128)(2,1)S(1)} %get-tuple-element.14.far, f32[3072,256]{1,0:T(8,128)S(1)} %get-tuple-element.15.pre, f32[256,256]{1,0:T(8,128)S(1)} %get-tuple-element.16.node_pre, ...), custom_call_target="tpu_custom_call" | custom-call | tf_op jit(solution)/shard_map/pallas_call | solution.py:384

commit v4 on v3

--- a/solution.py
+++ b/solution.py
@@ -12,6 +12,7 @@
 MESH = pl.DeviceIdType.MESH
 LANES = 128
 CHUNK = 512
+AHEAD = 4
 
 
 def dot(a, b):
@@ -61,10 +62,10 @@
 def exchange(
     n_lat,
     n_lon,
+    rim_index_in,
     nodes_in,
     w1_in,
     send_index_in,
-    rim_index_in,
     senders_in,
     b1_in,
     c1_in,
@@ -75,26 +76,28 @@
     ngain_in,
     v1_in,
     edges_in,
-    far,
+    rims_far,
+    marks_far,
+    member,
     pre,
     node_pre,
     w2c,
     v2c,
-    sender_turned,
     nodes,
-    receivers,
     gain,
     ngain,
     v1,
     edges,
+    rim_index,
     w1,
     send_index,
-    rim_index,
     senders,
     b1,
     c1,
     w2,
     v2,
+    receivers,
+    band_far,
     outgoing,
     load_sem,
     send_sem,
@@ -104,7 +107,8 @@
     node_rows, width = nodes.shape
     halo = send_index.shape[1]
     rim = rim_index.shape[1]
-    rim_at = n_lon * halo
+    rim_from = node_rows + n_lon * halo
+    rim_to = rim_from + 2 * rim
     chunks = edges.shape[0] // CHUNK
     blocks = CHUNK // LANES
 
@@ -122,63 +126,84 @@
     def _():
         pl.semaphore_signal(barrier, inc=1, device_id=(a + 1, b), device_id_type=MESH)
 
+    sender_rows = pl.ds(width, width)
     pairs = [
+        (rim_index_in, rim_index),
         (nodes_in, nodes),
-        (w1_in, w1),
+        (w1_in.at[sender_rows], w1.at[sender_rows]),
         (send_index_in, send_index),
-        (rim_index_in, rim_index),
         (senders_in, senders),
+        (receivers_in, receivers),
+        (w1_in.at[pl.ds(0, width)], w1.at[pl.ds(0, width)]),
+        (w1_in.at[pl.ds(2 * width, width)], w1.at[pl.ds(2 * width, width)]),
         (b1_in, b1),
+        (edges_in, edges),
         (c1_in, c1),
         (w2_in, w2),
         (v2_in, v2),
-        (receivers_in, receivers),
         (gain_in, gain),
         (ngain_in, ngain),
         (v1_in, v1),
-        (edges_in, edges),
     ]
     loads = [
         pltpu.make_async_copy(src, dst, load_sem.at[i]) for i, (src, dst) in enumerate(pairs)
     ]
     for copy in loads:
         copy.start()
+
+    @pl.when(a == 0)
+    def _():
+        rims_far[:rim] = jnp.zeros((rim, width), BF16)
+
+    @pl.when(a == n_lat - 1)
+    def _():
+        rims_far[rim:] = jnp.zeros((rim, width), BF16)
+
     for copy in loads[:4]:
         copy.wait()
-
     lists = jnp.concatenate(
         [send_index[...], jnp.zeros((n_lon, LANES - halo), jnp.int32)], axis=1
     )
     list_turned = turned(jnp.concatenate([rim_index[...], lists], axis=0))
     own = nodes[...]
-    by_sender = (0.5 * dot(own, w1[width : 2 * width])).astype(BF16)
-    for p in range(n_lon):
-        chosen = pick_rows(list_turned[:halo, 2 + p : 3 + p], 0, node_rows)
-        outgoing[p * halo : (p + 1) * halo] = dot(chosen, by_sender).astype(BF16)
-    for side in range(2):
-        chosen = pick_rows(list_turned[:, side : side + 1], 0, node_rows)
-        at = n_lon * halo + side * rim
-        outgoing[at : at + rim] = dot(chosen, by_sender).astype(BF16)
-    mine = pl.multiple_of(b * halo, halo)
-    far[pl.ds(mine, halo)] = outgoing[pl.ds(mine, halo)]
-
-    @pl.when(a == 0)
-    def _():
-        far[rim_at : rim_at + rim] = jnp.zeros((rim, width), BF16)
-
-    @pl.when(a == n_lat - 1)
-    def _():
-        far[rim_at + rim :] = jnp.zeros((rim, width), BF16)
+    by_sender = (0.5 * dot(own, w1[sender_rows])).astype(BF16)
+    chosen = [pick_rows(list_turned[:, side : side + 1], 0, node_rows) for side in range(2)]
+    outgoing[: 2 * rim] = dot(jnp.concatenate(chosen, axis=0), by_sender).astype(BF16)
 
     below = jnp.where(a > 0, 1, 0)
     above = jnp.where(a < n_lat - 1, 1, 0)
     pl.semaphore_wait(barrier, n_lon - 1 + below + above)
+    rims = [
+        pltpu.make_async_remote_copy(
+            src_ref=outgoing.at[pl.ds(side * rim, rim)],
+            dst_ref=rims_far.at[pl.ds(side * rim, rim)],
+            send_sem=send_sem.at[n_lon - 1 + side],
+            recv_sem=recv_sem.at[n_lon - 1 + side],
+            device_id=(a + 1 - 2 * side, b),
+            device_id_type=MESH,
+        )
+        for side in range(2)
+    ]
+
+    @pl.when(a < n_lat - 1)
+    def _():
+        rims[0].start()
+
+    @pl.when(a > 0)
+    def _():
+        rims[1].start()
+
+    chosen = [
+        pick_rows(list_turned[:halo, 2 + p : 3 + p], 0, node_rows) for p in range(n_lon)
+    ]
+    outgoing[2 * rim :] = dot(jnp.concatenate(chosen, axis=0), by_sender).astype(BF16)
+    mine = pl.multiple_of(b * halo, halo)
     band = []
     for d in range(1, n_lon):
         p = lax.rem(b + d, n_lon)
         copy = pltpu.make_async_remote_copy(
-            src_ref=outgoing.at[pl.ds(pl.multiple_of(p * halo, halo), halo)],
-            dst_ref=far.at[pl.ds(mine, halo)],
+            src_ref=outgoing.at[pl.ds(2 * rim + pl.multiple_of(p * halo, halo), halo)],
+            dst_ref=band_far.at[pl.ds(mine, halo)],
             send_sem=send_sem.at[d - 1],
             recv_sem=recv_sem.at[d - 1],
             device_id=(a, p),
@@ -186,54 +211,58 @@
         )
         copy.start()
         band.append(copy)
-    rims = [
-        pltpu.make_async_remote_copy(
-            src_ref=outgoing.at[pl.ds(n_lon * halo + side * rim, rim)],
-            dst_ref=far.at[pl.ds(rim_at + side * rim, rim)],
-            send_sem=send_sem.at[n_lon - 1 + side],
-            recv_sem=recv_sem.at[n_lon - 1 + side],
-            device_id=(a + 1 - 2 * side, b),
-            device_id_type=MESH,
-        )
-        for side in range(2)
-    ]
-
-    @pl.when(a < n_lat - 1)
-    def _():
-        rims[0].start()
-
-    @pl.when(a > 0)
-    def _():
-        rims[1].start()
+    band_far[pl.ds(mine, halo)] = outgoing[pl.ds(2 * rim + mine, halo)]
 
     for copy in loads[4:]:
         copy.wait()
-    sender_turned[...] = turned(senders[...])
+    sender_turned = turned(senders[...])
     receiver_turned = turned(receivers[...])
     by_receiver = (0.5 * (dot(own, w1[2 * width :]) + b1[...])).astype(BF16)
     near = jnp.concatenate(
         [(0.5 * w1[:width].astype(F32)).astype(BF16), by_receiver, by_sender], axis=0
     )
-    for i in range(chunks):
-        span = slice(i * CHUNK, (i + 1) * CHUNK)
-        marks = [
-            jnp.concatenate(
-                [
-                    pick_rows(receiver_turned[:, j : j + 1], 0, node_rows),
-                    pick_rows(sender_turned[:, j : j + 1], 0, node_rows),
-                ],
-                axis=1,
-            )
+
+    def marks(turned_rows, i, low, high):
+        rows = [
+            pick_rows(turned_rows[:, j : j + 1], low, high)
             for j in range(i * blocks, (i + 1) * blocks)
         ]
-        marks = jnp.concatenate(marks, axis=0)
-        pre[span] = dot(jnp.concatenate([edges[span], marks], axis=1), near)
+        return jnp.concatenate(rows, axis=0)
+
+    def near_part(i):
+        span = slice(i * CHUNK, (i + 1) * CHUNK)
+        marks_far[span] = marks(sender_turned, i, rim_from, rim_to)
+        row = [
+            mark(jnp.broadcast_to(receivers[j : j + 1], ids.shape).astype(jnp.int16) == ids)
+            for j in range(i * blocks, (i + 1) * blocks)
+        ]
+        member[:, span] = jnp.concatenate(row, axis=1)
+        rows = [
+            edges[span],
+            marks(receiver_turned, i, 0, node_rows),
+            marks(sender_turned, i, 0, node_rows),
+        ]
+        return rows
+
+    ids = row_ids(node_rows)
+    ahead = min(AHEAD, chunks)
+    for i in range(ahead):
+        pre[i * CHUNK : (i + 1) * CHUNK] = dot(jnp.concatenate(near_part(i), axis=1), near)
     w2c[...] = centred_weights(w2[...])
     v2c[...] = centred_weights(v2[...])
     node_pre[...] = 0.5 * (dot(own, v1[:width]) + c1[...])
 
     for copy in band:
         copy.wait()
+    from_band = band_far[...]
+    for i in range(ahead):
+        pre[i * CHUNK : (i + 1) * CHUNK] += dot(
+            marks(sender_turned, i, node_rows, rim_from), from_band
+        )
+    wide = jnp.concatenate([near, from_band], axis=0)
+    for i in range(ahead, chunks):
+        rows = near_part(i) + [marks(sender_turned, i, node_rows, rim_from)]
+        pre[i * CHUNK : (i + 1) * CHUNK] = dot(jnp.concatenate(rows, axis=1), wide)
 
     @pl.when(a < n_lat - 1)
     def _():
@@ -248,14 +277,14 @@
 
 def finish(
     count,
-    far,
+    rims_far,
+    marks_far,
+    member,
     pre,
     node_pre,
     w2c,
     v2c,
-    sender_turned,
     nodes,
-    receivers,
     gain,
     ngain,
     v1,
@@ -268,19 +297,13 @@
 ):
     node_rows, width = nodes.shape
     chunks = edges.shape[0] // CHUNK
-    blocks = CHUNK // LANES
     ones = jnp.full((width, LANES), 1.0 / width, BF16)
     live = count[0]
     messages = jnp.zeros((node_rows, width), F32)
-    ids = row_ids(node_rows)
     stores = []
     for i in range(chunks):
         span = slice(i * CHUNK, (i + 1) * CHUNK)
-        marks = [
-            pick_rows(sender_turned[:, j : j + 1], node_rows, node_rows + far.shape[0])
-            for j in range(i * blocks, (i + 1) * blocks)
-        ]
-        hidden = halved_silu(pre[span] + dot(jnp.concatenate(marks, axis=0), far[...]))
+        hidden = halved_silu(pre[span] + dot(marks_far[span], rims_far[...]))
         y = dot(hidden, w2c[...])
         scale = inverse_spread(y, ones)
         slot = lax.broadcasted_iota(jnp.int32, scale.shape, 0) + i * CHUNK
@@ -291,11 +314,7 @@
         copy = pltpu.make_async_copy(fresh.at[span], new_edges.at[span], store_sem.at[i])
         copy.start()
         stores.append(copy)
-        member = [
-            mark(jnp.broadcast_to(receivers[j : j + 1], ids.shape).astype(jnp.int16) == ids)
-            for j in range(i * blocks, (i + 1) * blocks)
-        ]
-        messages = messages + dot(jnp.concatenate(member, axis=1), update)
+        messages = messages + dot(member[:, span], update)
 
     h = node_pre[...] + 0.5 * dot(messages.astype(BF16), v1[width:])
     z = dot(halved_silu(h), v2c[...])
@@ -332,35 +351,38 @@
     node_gain,
 ):
     width = nodes.shape[1]
-    listed = n_lon * send_index.shape[1] + 2 * rim_index.shape[1]
     inner = (
+        rim_index,
         nodes,
         edge_w1,
         send_index,
-        rim_index,
         senders.reshape(-1, LANES),
         edge_b1.reshape(1, width),
         node_b1.reshape(1, width),
         edge_w2,
         node_w2,
+        receivers.reshape(-1, LANES),
     )
     passed = (
-        receivers.reshape(-1, LANES),
         edge_gain.reshape(1, width),
         node_gain.reshape(1, width),
         node_w1,
         edges,
     )
     operands = [in_hbm(x) for x in inner + passed]
+    node_rows, edge_rows = nodes.shape[0], edges.shape[0]
+    band_rows, rim_rows = n_lon * send_index.shape[1], 2 * rim_index.shape[1]
     handed = [
-        ((listed, width), BF16),
+        ((rim_rows, width), BF16),
+        ((edge_rows, rim_rows), BF16),
+        ((node_rows, edge_rows), BF16),
         (edges.shape, F32),
         (nodes.shape, F32),
         (edge_w2.shape, BF16),
         (node_w2.shape, BF16),
-        ((LANES, LANES), jnp.int32),
         (nodes.shape, BF16),
     ] + [(x.shape, x.dtype) for x in passed]
+    scratch = [x for x in inner if x is not nodes]
     hbm = pl.BlockSpec(memory_space=pltpu.HBM)
     vmem = pl.BlockSpec(memory_space=pltpu.VMEM)
     limit = 24 * 1024 * 1024
@@ -369,10 +391,11 @@
         out_shape=tuple(pltpu.VMEM(shape, dtype) for shape, dtype in handed),
         in_specs=[hbm] * len(operands),
         out_specs=(vmem,) * len(handed),
-        scratch_shapes=[pltpu.VMEM(x.shape, x.dtype) for x in inner[1:]]
+        scratch_shapes=[pltpu.VMEM(x.shape, x.dtype) for x in scratch]
         + [
-            pltpu.VMEM((listed, width), BF16),
-            pltpu.SemaphoreType.DMA((len(operands),)),
+            pltpu.VMEM((band_rows, width), BF16),
+            pltpu.VMEM((rim_rows + band_rows, width), BF16),
+            pltpu.SemaphoreType.DMA((len(operands) + 2,)),
             pltpu.SemaphoreType.DMA((n_lon + 1,)),
             pltpu.SemaphoreType.DMA((n_lon + 1,)),
         ],

time: 13.1 us -> 13 us (level)
    pallas_call x1, Pallas kernels: 7.12 us -> 7.91 us  [local(): pl.pallas_call(functools.partial(exchange, n_lat, n_lon), out_shape=tuple...]
    pallas_call x1, Pallas kernels: 4.44 us -> 3.67 us  [local(): pl.pallas_call(finish, out_shape=(pltpu.HBM(nodes.shape, BF16), pltpu.HBM...]
where the time goes in v4:
time: 13 us; the launch traced here: 12.9 us
  Pallas kernels  11.6 us (89%)
  between operations  1.29 us (10%)
    pallas_call x1, Pallas kernels, local(): pl.pallas_call(functools.partial(exchange, n_lat, n_lon), out_shape=tuple...  7.91 us
    pallas_call x1, Pallas kernels, local(): pl.pallas_call(finish, out_shape=(pltpu.HBM(nodes.shape, BF16), pltpu.HBM...  3.67 us

profile of v4, /device:TPU:0, one launch (start us, length us, event | category | flops | bytes accessed | tf_op | source)
XLA Modules:
  0.0 12.9 jit_solution(2258419577898020009)
XLA Ops:
  1.3 7.9 %shard_map.158 = (bf16[256,256]{1,0:T(8,128)(2,1)S(1)}, bf16[3072,256]{1,0:T(8,128)(2,1)S(1)}, bf16[256,3072]{1,0:T(8,128)(2,1)S(1)}, f32[3072,256]{1,0:T(8,128)...) custom-call(s32[2,128]{1,0:T(2,128)} %rim_index_in.1, ...), custom_call_target="tpu_custom_call" | custom-call | tf_op jit(solution)/shard_map/pallas_call | solution.py:389
  9.2 3.7 %shard_map.159 = (bf16[256,256]{1,0:T(8,128)(2,1)}, bf16[3072,256]{1,0:T(8,128)(2,1)}) custom-call(s32[1]{0:T(128)S(6)} %copy.17.count, bf16[256,256]{1,0:T(8,128)(2,1)S(1)} %get-tuple-element.14.rims_far, bf16[3072,256]{1,0:T(8,128)(2,1)S(1)} %get-tuple-element.15.marks_far, bf16[256,3072]{1,0:T(8,128)(2,1)S(1)} %get-tuple-element.16.member, ...), custom_call_target="tpu_custom_call" | custom-call | tf_op jit(solution)/shard_map/pallas_call | solution.py:407

commit v5 on v4

--- a/solution.py
+++ b/solution.py
@@ -12,6 +12,7 @@
 MESH = pl.DeviceIdType.MESH
 LANES = 128
 CHUNK = 512
+STEP = 256
 AHEAD = 4
 
 
@@ -170,6 +171,22 @@
     chosen = [pick_rows(list_turned[:, side : side + 1], 0, node_rows) for side in range(2)]
     outgoing[: 2 * rim] = dot(jnp.concatenate(chosen, axis=0), by_sender).astype(BF16)
 
+    chosen = [
+        pick_rows(list_turned[:halo, 2 + p : 3 + p], 0, node_rows) for p in range(n_lon)
+    ]
+    outgoing[2 * rim :] = dot(jnp.concatenate(chosen, axis=0), by_sender).astype(BF16)
+    for copy in loads[4:]:
+        copy.wait()
+    sender_turned = turned(senders[...])
+    receiver_turned = turned(receivers[...])
+    by_receiver = (0.5 * (dot(own, w1[2 * width :]) + b1[...])).astype(BF16)
+    near = jnp.concatenate(
+        [(0.5 * w1[:width].astype(F32)).astype(BF16), by_receiver, by_sender], axis=0
+    )
+    w2c[...] = centred_weights(w2[...])
+    v2c[...] = centred_weights(v2[...])
+    node_pre[...] = 0.5 * (dot(own, v1[:width]) + c1[...])
+
     below = jnp.where(a > 0, 1, 0)
     above = jnp.where(a < n_lat - 1, 1, 0)
     pl.semaphore_wait(barrier, n_lon - 1 + below + above)
@@ -193,10 +210,6 @@
     def _():
         rims[1].start()
 
-    chosen = [
-        pick_rows(list_turned[:halo, 2 + p : 3 + p], 0, node_rows) for p in range(n_lon)
-    ]
-    outgoing[2 * rim :] = dot(jnp.concatenate(chosen, axis=0), by_sender).astype(BF16)
     mine = pl.multiple_of(b * halo, halo)
     band = []
     for d in range(1, n_lon):
@@ -213,15 +226,6 @@
         band.append(copy)
     band_far[pl.ds(mine, halo)] = outgoing[pl.ds(2 * rim + mine, halo)]
 
-    for copy in loads[4:]:
-        copy.wait()
-    sender_turned = turned(senders[...])
-    receiver_turned = turned(receivers[...])
-    by_receiver = (0.5 * (dot(own, w1[2 * width :]) + b1[...])).astype(BF16)
-    near = jnp.concatenate(
-        [(0.5 * w1[:width].astype(F32)).astype(BF16), by_receiver, by_sender], axis=0
-    )
-
     def marks(turned_rows, i, low, high):
         rows = [
             pick_rows(turned_rows[:, j : j + 1], low, high)
@@ -248,10 +252,6 @@
     ahead = min(AHEAD, chunks)
     for i in range(ahead):
         pre[i * CHUNK : (i + 1) * CHUNK] = dot(jnp.concatenate(near_part(i), axis=1), near)
-    w2c[...] = centred_weights(w2[...])
-    v2c[...] = centred_weights(v2[...])
-    node_pre[...] = 0.5 * (dot(own, v1[:width]) + c1[...])
-
     for copy in band:
         copy.wait()
     from_band = band_far[...]
@@ -296,17 +296,17 @@
     store_sem,
 ):
     node_rows, width = nodes.shape
-    chunks = edges.shape[0] // CHUNK
+    chunks = edges.shape[0] // STEP
     ones = jnp.full((width, LANES), 1.0 / width, BF16)
     live = count[0]
     messages = jnp.zeros((node_rows, width), F32)
     stores = []
     for i in range(chunks):
-        span = slice(i * CHUNK, (i + 1) * CHUNK)
+        span = slice(i * STEP, (i + 1) * STEP)
         hidden = halved_silu(pre[span] + dot(marks_far[span], rims_far[...]))
         y = dot(hidden, w2c[...])
         scale = inverse_spread(y, ones)
-        slot = lax.broadcasted_iota(jnp.int32, scale.shape, 0) + i * CHUNK
+        slot = lax.broadcasted_iota(jnp.int32, scale.shape, 0) + i * STEP
         scale = jnp.where(slot < live, scale, 0.0)
         scale = jnp.concatenate([scale] * (width // LANES), axis=1)
         update = (y * scale * gain[...]).astype(BF16)
@@ -403,7 +403,7 @@
             collective_id=0, has_side_effects=True, vmem_limit_bytes=limit
         ),
     )(*operands)
-    chunks = edges.shape[0] // CHUNK
+    chunks = edges.shape[0] // STEP
     return pl.pallas_call(
         finish,
         out_shape=(pltpu.HBM(nodes.shape, BF16), pltpu.HBM(edges.shape, BF16)),

time: 13 us -> 14.7 us (1.13)
  Pallas kernels: 11.6 us -> 13.2 us
    pallas_call x1, Pallas kernels: 3.67 us -> 4.9 us  [local(): pl.pallas_call(finish, out_shape=(pltpu.HBM(nodes.shape, BF16), pltpu.HBM...]
    pallas_call x1, Pallas kernels: 7.91 us -> 8.3 us  [local(): pl.pallas_call(functools.partial(exchange, n_lat, n_lon), out_shape=tuple...]
where the time goes in v5:
time: 14.7 us; the launch traced here: 14.5 us
  Pallas kernels  13.2 us (90%)
  between operations  1.29 us (9%)
    pallas_call x1, Pallas kernels, local(): pl.pallas_call(functools.partial(exchange, n_lat, n_lon), out_shape=tuple...  8.3 us
    pallas_call x1, Pallas kernels, local(): pl.pallas_call(finish, out_shape=(pltpu.HBM(nodes.shape, BF16), pltpu.HBM...  4.9 us

profile of v5, /device:TPU:0, one launch (start us, length us, event | category | flops | bytes accessed | tf_op | source)
XLA Modules:
  0.0 14.5 jit_solution(15655212104177917962)
XLA Ops:
  1.3 8.3 %shard_map.158 = (bf16[256,256]{1,0:T(8,128)(2,1)S(1)}, bf16[3072,256]{1,0:T(8,128)(2,1)S(1)}, bf16[256,3072]{1,0:T(8,128)(2,1)S(1)}, f32[3072,256]{1,0:T(8,128)...) custom-call(s32[2,128]{1,0:T(2,128)} %rim_index_in.1, ...), custom_call_target="tpu_custom_call" | custom-call | tf_op jit(solution)/shard_map/pallas_call | solution.py:389
  9.6 4.9 %shard_map.159 = (bf16[256,256]{1,0:T(8,128)(2,1)}, bf16[3072,256]{1,0:T(8,128)(2,1)}) custom-call(s32[1]{0:T(128)S(6)} %copy.17.count, bf16[256,256]{1,0:T(8,128)(2,1)S(1)} %get-tuple-element.14.rims_far, bf16[3072,256]{1,0:T(8,128)(2,1)S(1)} %get-tuple-element.15.marks_far, bf16[256,3072]{1,0:T(8,128)(2,1)S(1)} %get-tuple-element.16.member, ...), custom_call_target="tpu_custom_call" | custom-call | tf_op jit(solution)/shard_map/pallas_call | solution.py:407

commit v6 on v4

--- a/solution.py
+++ b/solution.py
@@ -11,8 +11,8 @@
 F32 = jnp.float32
 MESH = pl.DeviceIdType.MESH
 LANES = 128
-CHUNK = 512
-AHEAD = 4
+CHUNK = 1024
+AHEAD = 2
 
 
 def dot(a, b):
@@ -300,7 +300,6 @@
     ones = jnp.full((width, LANES), 1.0 / width, BF16)
     live = count[0]
     messages = jnp.zeros((node_rows, width), F32)
-    stores = []
     for i in range(chunks):
         span = slice(i * CHUNK, (i + 1) * CHUNK)
         hidden = halved_silu(pre[span] + dot(marks_far[span], rims_far[...]))
@@ -311,20 +310,19 @@
         scale = jnp.concatenate([scale] * (width // LANES), axis=1)
         update = (y * scale * gain[...]).astype(BF16)
         fresh[span] = edges[span] + update
-        copy = pltpu.make_async_copy(fresh.at[span], new_edges.at[span], store_sem.at[i])
-        copy.start()
-        stores.append(copy)
         messages = messages + dot(member[:, span], update)
 
+    edge_store = pltpu.make_async_copy(fresh, new_edges, store_sem.at[0])
+    edge_store.start()
     h = node_pre[...] + 0.5 * dot(messages.astype(BF16), v1[width:])
     z = dot(halved_silu(h), v2c[...])
     scale = inverse_spread(z, ones)
     scale = jnp.concatenate([scale] * (width // LANES), axis=1)
     fresh_nodes[...] = (nodes[...].astype(F32) + z * scale * ngain[...]).astype(BF16)
-    copy = pltpu.make_async_copy(fresh_nodes, new_nodes, store_sem.at[chunks])
-    copy.start()
-    for copy in stores + [copy]:
-        copy.wait()
+    node_store = pltpu.make_async_copy(fresh_nodes, new_nodes, store_sem.at[1])
+    node_store.start()
+    edge_store.wait()
+    node_store.wait()
 
 
 def in_hbm(x):
@@ -403,7 +401,6 @@
             collective_id=0, has_side_effects=True, vmem_limit_bytes=limit
         ),
     )(*operands)
-    chunks = edges.shape[0] // CHUNK
     return pl.pallas_call(
         finish,
         out_shape=(pltpu.HBM(nodes.shape, BF16), pltpu.HBM(edges.shape, BF16)),
@@ -412,7 +409,7 @@
         scratch_shapes=[
             pltpu.VMEM(edges.shape, BF16),
             pltpu.VMEM(nodes.shape, BF16),
-            pltpu.SemaphoreType.DMA((chunks + 1,)),
+            pltpu.SemaphoreType.DMA((2,)),
         ],
         compiler_params=pltpu.CompilerParams(vmem_limit_bytes=limit),
     )(edge_count, *between)

time: 13 us -> 13.3 us (1.023)
  Pallas kernels: 11.6 us -> 11.8 us
    pallas_call x1, Pallas kernels: 7.91 us -> 8.43 us  [local(): pl.pallas_call(functools.partial(exchange, n_lat, n_lon), out_shape=tuple...]
    pallas_call x1, Pallas kernels: 3.67 us -> 3.4 us  [local(): pl.pallas_call(finish, out_shape=(pltpu.HBM(nodes.shape, BF16), pltpu.HBM...]
where the time goes in v6:
time: 13.3 us; the launch traced here: 13.1 us
  Pallas kernels  11.8 us (89%)
  between operations  1.29 us (10%)
    pallas_call x1, Pallas kernels, local(): pl.pallas_call(functools.partial(exchange, n_lat, n_lon), out_shape=tuple...  8.43 us
    pallas_call x1, Pallas kernels, local(): pl.pallas_call(finish, out_shape=(pltpu.HBM(nodes.shape, BF16), pltpu.HBM...  3.4 us

profile of v6, /device:TPU:0, one launch (start us, length us, event | category | flops | bytes accessed | tf_op | source)
XLA Modules:
  0.0 13.1 jit_solution(14124592894526707692)
XLA Ops:
  1.3 8.4 %shard_map.158 = (bf16[256,256]{1,0:T(8,128)(2,1)S(1)}, bf16[3072,256]{1,0:T(8,128)(2,1)S(1)}, bf16[256,3072]{1,0:T(8,128)(2,1)S(1)}, f32[3072,256]{1,0:T(8,128)...) custom-call(s32[2,128]{1,0:T(2,128)} %rim_index_in.1, ...), custom_call_target="tpu_custom_call" | custom-call | tf_op jit(solution)/shard_map/pallas_call | solution.py:387
  9.7 3.4 %shard_map.159 = (bf16[256,256]{1,0:T(8,128)(2,1)}, bf16[3072,256]{1,0:T(8,128)(2,1)}) custom-call(s32[1]{0:T(128)S(6)} %copy.17.count, bf16[256,256]{1,0:T(8,128)(2,1)S(1)} %get-tuple-element.14.rims_far, bf16[3072,256]{1,0:T(8,128)(2,1)S(1)} %get-tuple-element.15.marks_far, bf16[256,3072]{1,0:T(8,128)(2,1)S(1)} %get-tuple-element.16.member, ...), custom_call_target="tpu_custom_call" | custom-call | tf_op jit(solution)/shard_map/pallas_call | solution.py:404

commit v7 on v6

--- a/solution.py
+++ b/solution.py
@@ -11,8 +11,8 @@
 F32 = jnp.float32
 MESH = pl.DeviceIdType.MESH
 LANES = 128
-CHUNK = 1024
-AHEAD = 2
+CHUNK = 512
+STEP = 1024
 
 
 def dot(a, b):
@@ -76,7 +76,7 @@
     ngain_in,
     v1_in,
     edges_in,
-    rims_far,
+    far,
     marks_far,
     member,
     pre,
@@ -97,7 +97,6 @@
     w2,
     v2,
     receivers,
-    band_far,
     outgoing,
     load_sem,
     send_sem,
@@ -107,8 +106,8 @@
     node_rows, width = nodes.shape
     halo = send_index.shape[1]
     rim = rim_index.shape[1]
-    rim_from = node_rows + n_lon * halo
-    rim_to = rim_from + 2 * rim
+    halos = n_lon * halo
+    table_rows = node_rows + halos + 2 * rim
     chunks = edges.shape[0] // CHUNK
     blocks = CHUNK // LANES
 
@@ -153,11 +152,11 @@
 
     @pl.when(a == 0)
     def _():
-        rims_far[:rim] = jnp.zeros((rim, width), BF16)
+        far[halos : halos + rim] = jnp.zeros((rim, width), BF16)
 
     @pl.when(a == n_lat - 1)
     def _():
-        rims_far[rim:] = jnp.zeros((rim, width), BF16)
+        far[halos + rim :] = jnp.zeros((rim, width), BF16)
 
     for copy in loads[:4]:
         copy.wait()
@@ -176,7 +175,7 @@
     rims = [
         pltpu.make_async_remote_copy(
             src_ref=outgoing.at[pl.ds(side * rim, rim)],
-            dst_ref=rims_far.at[pl.ds(side * rim, rim)],
+            dst_ref=far.at[pl.ds(halos + side * rim, rim)],
             send_sem=send_sem.at[n_lon - 1 + side],
             recv_sem=recv_sem.at[n_lon - 1 + side],
             device_id=(a + 1 - 2 * side, b),
@@ -203,7 +202,7 @@
         p = lax.rem(b + d, n_lon)
         copy = pltpu.make_async_remote_copy(
             src_ref=outgoing.at[pl.ds(2 * rim + pl.multiple_of(p * halo, halo), halo)],
-            dst_ref=band_far.at[pl.ds(mine, halo)],
+            dst_ref=far.at[pl.ds(mine, halo)],
             send_sem=send_sem.at[d - 1],
             recv_sem=recv_sem.at[d - 1],
             device_id=(a, p),
@@ -211,7 +210,7 @@
         )
         copy.start()
         band.append(copy)
-    band_far[pl.ds(mine, halo)] = outgoing[pl.ds(2 * rim + mine, halo)]
+    far[pl.ds(mine, halo)] = outgoing[pl.ds(2 * rim + mine, halo)]
 
     for copy in loads[4:]:
         copy.wait()
@@ -231,7 +230,7 @@
 
     def near_part(i):
         span = slice(i * CHUNK, (i + 1) * CHUNK)
-        marks_far[span] = marks(sender_turned, i, rim_from, rim_to)
+        marks_far[span] = marks(sender_turned, i, node_rows, table_rows)
         row = [
             mark(jnp.broadcast_to(receivers[j : j + 1], ids.shape).astype(jnp.int16) == ids)
             for j in range(i * blocks, (i + 1) * blocks)
@@ -245,8 +244,7 @@
         return rows
 
     ids = row_ids(node_rows)
-    ahead = min(AHEAD, chunks)
-    for i in range(ahead):
+    for i in range(chunks):
         pre[i * CHUNK : (i + 1) * CHUNK] = dot(jnp.concatenate(near_part(i), axis=1), near)
     w2c[...] = centred_weights(w2[...])
     v2c[...] = centred_weights(v2[...])
@@ -254,15 +252,6 @@
 
     for copy in band:
         copy.wait()
-    from_band = band_far[...]
-    for i in range(ahead):
-        pre[i * CHUNK : (i + 1) * CHUNK] += dot(
-            marks(sender_turned, i, node_rows, rim_from), from_band
-        )
-    wide = jnp.concatenate([near, from_band], axis=0)
-    for i in range(ahead, chunks):
-        rows = near_part(i) + [marks(sender_turned, i, node_rows, rim_from)]
-        pre[i * CHUNK : (i + 1) * CHUNK] = dot(jnp.concatenate(rows, axis=1), wide)
 
     @pl.when(a < n_lat - 1)
     def _():
@@ -277,7 +266,7 @@
 
 def finish(
     count,
-    rims_far,
+    far,
     marks_far,
     member,
     pre,
@@ -296,16 +285,16 @@
     store_sem,
 ):
     node_rows, width = nodes.shape
-    chunks = edges.shape[0] // CHUNK
+    chunks = edges.shape[0] // STEP
     ones = jnp.full((width, LANES), 1.0 / width, BF16)
     live = count[0]
     messages = jnp.zeros((node_rows, width), F32)
     for i in range(chunks):
-        span = slice(i * CHUNK, (i + 1) * CHUNK)
-        hidden = halved_silu(pre[span] + dot(marks_far[span], rims_far[...]))
+        span = slice(i * STEP, (i + 1) * STEP)
+        hidden = halved_silu(pre[span] + dot(marks_far[span], far[...]))
         y = dot(hidden, w2c[...])
         scale = inverse_spread(y, ones)
-        slot = lax.broadcasted_iota(jnp.int32, scale.shape, 0) + i * CHUNK
+        slot = lax.broadcasted_iota(jnp.int32, scale.shape, 0) + i * STEP
         scale = jnp.where(slot < live, scale, 0.0)
         scale = jnp.concatenate([scale] * (width // LANES), axis=1)
         update = (y * scale * gain[...]).astype(BF16)
@@ -369,10 +358,10 @@
     )
     operands = [in_hbm(x) for x in inner + passed]
     node_rows, edge_rows = nodes.shape[0], edges.shape[0]
-    band_rows, rim_rows = n_lon * send_index.shape[1], 2 * rim_index.shape[1]
+    listed = n_lon * send_index.shape[1] + 2 * rim_index.shape[1]
     handed = [
-        ((rim_rows, width), BF16),
-        ((edge_rows, rim_rows), BF16),
+        ((listed, width), BF16),
+        ((edge_rows, listed), BF16),
         ((node_rows, edge_rows), BF16),
         (edges.shape, F32),
         (nodes.shape, F32),
@@ -391,8 +380,7 @@
         out_specs=(vmem,) * len(handed),
         scratch_shapes=[pltpu.VMEM(x.shape, x.dtype) for x in scratch]
         + [
-            pltpu.VMEM((band_rows, width), BF16),
-            pltpu.VMEM((rim_rows + band_rows, width), BF16),
+            pltpu.VMEM((listed, width), BF16),
             pltpu.SemaphoreType.DMA((len(operands) + 2,)),
             pltpu.SemaphoreType.DMA((n_lon + 1,)),
             pltpu.SemaphoreType.DMA((n_lon + 1,)),

time: 13.3 us -> 12.5 us (0.940)
  Pallas kernels: 11.8 us -> 11 us
    pallas_call x1, Pallas kernels: 8.43 us -> 7.16 us  [local(): pl.pallas_call(functools.partial(exchange, n_lat, n_lon), out_shape=tuple...]
    pallas_call x1, Pallas kernels: 3.4 us -> 3.87 us  [local(): pl.pallas_call(finish, out_shape=(pltpu.HBM(nodes.shape, BF16), pltpu.HBM...]
where the time goes in v7:
time: 12.5 us; the launch traced here: 12.3 us
  Pallas kernels  11 us (88%)
  between operations  1.29 us (10%)
    pallas_call x1, Pallas kernels, local(): pl.pallas_call(functools.partial(exchange, n_lat, n_lon), out_shape=tuple...  7.16 us
    pallas_call x1, Pallas kernels, local(): pl.pallas_call(finish, out_shape=(pltpu.HBM(nodes.shape, BF16), pltpu.HBM...  3.87 us

profile of v7, /device:TPU:0, one launch (start us, length us, event | category | flops | bytes accessed | tf_op | source)
XLA Modules:
  0.0 12.3 jit_solution(4633004214421945784)
XLA Ops:
  1.3 7.2 %shard_map.158 = (bf16[512,256]{1,0:T(8,128)(2,1)S(1)}, bf16[3072,512]{1,0:T(8,128)(2,1)S(1)}, bf16[256,3072]{1,0:T(8,128)(2,1)S(1)}, f32[3072,256]{1,0:T(8,128)...) custom-call(s32[2,128]{1,0:T(2,128)} %rim_index_in.1, ...), custom_call_target="tpu_custom_call" | custom-call | tf_op jit(solution)/shard_map/pallas_call | solution.py:376
  8.4 3.9 %shard_map.159 = (bf16[256,256]{1,0:T(8,128)(2,1)}, bf16[3072,256]{1,0:T(8,128)(2,1)}) custom-call(s32[1]{0:T(128)S(6)} %copy.17.count, bf16[512,256]{1,0:T(8,128)(2,1)S(1)} %get-tuple-element.14.far, bf16[3072,512]{1,0:T(8,128)(2,1)S(1)} %get-tuple-element.15.marks_far, bf16[256,3072]{1,0:T(8,128)(2,1)S(1)} %get-tuple-element.16.member, ...), custom_call_target="tpu_custom_call" | custom-call | tf_op jit(solution)/shard_map/pallas_call | solution.py:392

commit v8 on v7

--- a/solution.py
+++ b/solution.py
@@ -12,7 +12,7 @@
 MESH = pl.DeviceIdType.MESH
 LANES = 128
 CHUNK = 512
-STEP = 1024
+STEP = 1536
 
 
 def dot(a, b):
@@ -111,20 +111,6 @@
     chunks = edges.shape[0] // CHUNK
     blocks = CHUNK // LANES
 
-    barrier = pltpu.get_barrier_semaphore()
-    for d in range(1, n_lon):
-        pl.semaphore_signal(
-            barrier, inc=1, device_id=(a, lax.rem(b + d, n_lon)), device_id_type=MESH
-        )
-
-    @pl.when(a > 0)
-    def _():
-        pl.semaphore_signal(barrier, inc=1, device_id=(a - 1, b), device_id_type=MESH)
-
-    @pl.when(a < n_lat - 1)
-    def _():
-        pl.semaphore_signal(barrier, inc=1, device_id=(a + 1, b), device_id_type=MESH)
-
     sender_rows = pl.ds(width, width)
     pairs = [
         (rim_index_in, rim_index),
@@ -147,7 +133,24 @@
     loads = [
         pltpu.make_async_copy(src, dst, load_sem.at[i]) for i, (src, dst) in enumerate(pairs)
     ]
-    for copy in loads:
+    for copy in loads[:4]:
+        copy.start()
+
+    barrier = pltpu.get_barrier_semaphore()
+    for d in range(1, n_lon):
+        pl.semaphore_signal(
+            barrier, inc=1, device_id=(a, lax.rem(b + d, n_lon)), device_id_type=MESH
+        )
+
+    @pl.when(a > 0)
+    def _():
+        pl.semaphore_signal(barrier, inc=1, device_id=(a - 1, b), device_id_type=MESH)
+
+    @pl.when(a < n_lat - 1)
+    def _():
+        pl.semaphore_signal(barrier, inc=1, device_id=(a + 1, b), device_id_type=MESH)
+
+    for copy in loads[4:]:
         copy.start()
 
     @pl.when(a == 0)

time: 12.5 us -> 12.6 us (level)
  no operation moved by 1% of the time
where the time goes in v8:
time: 12.6 us; the launch traced here: 12.4 us
  Pallas kernels  11.1 us (88%)
  between operations  1.29 us (10%)
    pallas_call x1, Pallas kernels, local(): pl.pallas_call(functools.partial(exchange, n_lat, n_lon), out_shape=tuple...  7.16 us
    pallas_call x1, Pallas kernels, local(): pl.pallas_call(finish, out_shape=(pltpu.HBM(nodes.shape, BF16), pltpu.HBM...  3.94 us

profile of v8, /device:TPU:0, one launch (start us, length us, event | category | flops | bytes accessed | tf_op | source)
XLA Modules:
  0.0 12.4 jit_solution(13509124480061400334)
XLA Ops:
  1.3 7.2 %shard_map.158 = (bf16[512,256]{1,0:T(8,128)(2,1)S(1)}, bf16[3072,512]{1,0:T(8,128)(2,1)S(1)}, bf16[256,3072]{1,0:T(8,128)(2,1)S(1)}, f32[3072,256]{1,0:T(8,128)...) custom-call(s32[2,128]{1,0:T(2,128)} %rim_index_in.1, ...), custom_call_target="tpu_custom_call" | custom-call | tf_op jit(solution)/shard_map/pallas_call | solution.py:379
  8.4 3.9 %shard_map.159 = (bf16[256,256]{1,0:T(8,128)(2,1)}, bf16[3072,256]{1,0:T(8,128)(2,1)}) custom-call(s32[1]{0:T(128)S(6)} %copy.17.count, bf16[512,256]{1,0:T(8,128)(2,1)S(1)} %get-tuple-element.14.far, bf16[3072,512]{1,0:T(8,128)(2,1)S(1)} %get-tuple-element.15.marks_far, bf16[256,3072]{1,0:T(8,128)(2,1)S(1)} %get-tuple-element.16.member, ...), custom_call_target="tpu_custom_call" | custom-call | tf_op jit(solution)/shard_map/pallas_call | solution.py:395
